TPU v7x, 32 devices: a whole 2x2x4 slice. The times are simulated.
32 devices in a mesh: dom: 8 (over z, y), feat: 4 (over x, core).
Axes of the slice: x: 2, y: 2, z: 4, core: 2. Of those that a mesh axis runs over, the one named last changes fastest.
Arguments:
- features: bfloat16 [65536, 128], P(('dom', 'feat')), may hold values from -6 to 6
- grad_out: bfloat16 [65536, 256], P(('dom', 'feat')), may hold values from -6 to 6
- w_self: bfloat16 [128, 256], replicated, may hold values from -0.5 to 0.5
- w_neigh: bfloat16 [128, 256], replicated, may hold values from -2 to 2
- tile_src: int32 [512, 6], P(('dom', 'feat')), may hold values from 0 to 17, as said below
- tile_vals: int32 [3072, 128, 128], P(('dom', 'feat')), may hold values from 0 to 2
- send_rows: int32 [32, 128], P(('dom', 'feat')), may hold values from -1 to 2047, as said below
- hub_rows: int32 [32, 4], P(('dom', 'feat')), may hold values from 0 to 2047, as said below
Outputs:
- out_nodes: bfloat16 [65536, 256], P(('dom', 'feat'))
- grad_features: float32 [65536, 128], P(('dom', 'feat'))
- grad_w_self: float32 [128, 256], replicated
- grad_w_neigh: float32 [128, 256], replicated
Inputs may be any that keep to these rules, and one draw needn't show every extreme that they name: `tile_src`: the first 3 tiles of each row block name column blocks 0 to 15, the other 3 name blocks 16 to 17. `send_rows`: in each device's 4 slots toward one peer the used entries come first; every device fills all 4 slots toward at least one peer and at least one slot toward every peer. `hub_rows`: A device's hub rows are distinct.
All inputs are finite; a program needn't handle non-finite values.
Results may differ from a plain program's by a relative error of at most 0.0054.
Values may be sent and summed in bfloat16 or wider, within the bound.
A program may use at most 64 MiB of HBM per device.

v0:
```python
import jax
import jax.numpy as jnp
from jax import lax
from jax.sharding import PartitionSpec as P


def silu_slope(preact):
    sigma = jax.nn.sigmoid(preact)
    return sigma * (1.0 + preact * (1.0 - sigma))


def per_device(features, grad_out, w_self, w_neigh, tile_src, tile_vals, send_rows, hub_rows):
    n_dom = lax.axis_size("dom")
    n_feat = lax.axis_size("feat")
    node_dev, f_width = features.shape
    blocks, tiles = tile_src.shape
    block = tile_vals.shape[1]
    halo_rows = send_rows.shape[1]
    slots = halo_rows // (n_dom * n_feat)
    row_ids = send_rows[0]
    is_live = row_ids >= 0
    safe_ids = jnp.maximum(row_ids, 0)
    outgoing = jnp.where(is_live[:, None], features[safe_ids], jnp.zeros((), jnp.bfloat16))
    outgoing = outgoing.reshape(n_dom, n_feat, slots, f_width)
    sectioned = lax.all_to_all(outgoing, "feat", split_axis=1, concat_axis=1, tiled=True)
    arrived = lax.all_to_all(sectioned, "dom", split_axis=0, concat_axis=0, tiled=True)
    halo_block = arrived.reshape(halo_rows, f_width)
    hub_mine = features[hub_rows[0]]
    hub_all = lax.all_gather(hub_mine, ("dom", "feat"), axis=0, tiled=True)
    counts = tile_vals.reshape(blocks, tiles, block, block)
    weights_b = counts.astype(jnp.bfloat16)
    degree = jnp.sum(counts, axis=(1, 3)).astype(jnp.float32) + 1.0
    src_blocks = blocks + (halo_rows + hub_all.shape[0]) // block
    sources = jnp.concatenate([features, halo_block, hub_all], 0).reshape(
        src_blocks, block, f_width
    )
    summed = jnp.einsum(
        "btij,btjf->bif", weights_b, sources[tile_src], preferred_element_type=jnp.float32
    )
    neighbor = (summed / degree[:, :, None]).astype(jnp.bfloat16).reshape(node_dev, f_width)
    preact = jnp.dot(features, w_self, preferred_element_type=jnp.float32) + jnp.dot(
        neighbor, w_neigh, preferred_element_type=jnp.float32
    )
    output = jax.nn.silu(preact).astype(jnp.bfloat16)
    d_pre = (grad_out.astype(jnp.float32) * silu_slope(preact)).astype(jnp.bfloat16)
    over_rows = (((0,), (0,)), ((), ()))
    over_cols = (((1,), (1,)), ((), ()))
    dw_self = lax.dot_general(features, d_pre, over_rows, preferred_element_type=jnp.float32)
    dw_neigh = lax.dot_general(neighbor, d_pre, over_rows, preferred_element_type=jnp.float32)
    d_neigh = lax.dot_general(
        d_pre, w_neigh, over_cols, preferred_element_type=jnp.float32
    ).reshape(blocks, block, f_width)
    d_neigh = (d_neigh / degree[:, :, None]).astype(jnp.bfloat16)
    pieces = jnp.einsum("btij,bif->btjf", weights_b, d_neigh, preferred_element_type=jnp.float32)
    d_source = jax.ops.segment_sum(
        pieces.reshape(blocks * tiles, block, f_width),
        tile_src.reshape(-1),
        num_segments=src_blocks,
    )
    d_source = d_source.reshape(src_blocks * block, f_width)
    d_halo = (
        d_source[node_dev : node_dev + halo_rows]
        .astype(jnp.bfloat16)
        .reshape(n_dom, n_feat, slots, f_width)
    )
    sectioned_back = lax.all_to_all(d_halo, "feat", split_axis=1, concat_axis=1, tiled=True)
    returned = lax.all_to_all(sectioned_back, "dom", split_axis=0, concat_axis=0, tiled=True)
    returned = returned.reshape(halo_rows, f_width).astype(jnp.float32)
    returned = jnp.where(is_live[:, None], returned, jnp.zeros((), jnp.float32))
    hub_back = lax.psum_scatter(
        d_source[node_dev + halo_rows :], ("dom", "feat"), scatter_dimension=0, tiled=True
    )
    grad_feat = (
        lax.dot_general(d_pre, w_self, over_cols, preferred_element_type=jnp.float32)
        + d_source[:node_dev]
    )
    grad_feat = grad_feat + jax.ops.segment_sum(returned, safe_ids, num_segments=node_dev)
    grad_feat = grad_feat.at[hub_rows[0]].add(hub_back)
    weight_sums = lax.psum((dw_self, dw_neigh), ("dom", "feat"))
    return (output, grad_feat, weight_sums[0], weight_sums[1])


def solution(mesh):
    return jax.shard_map(
        per_device,
        mesh=mesh,
        in_specs=(
            P(("dom", "feat"), None),
            P(("dom", "feat"), None),
            P(),
            P(),
            P(("dom", "feat"), None),
            P(("dom", "feat"), None, None),
            P(("dom", "feat"), None),
            P(("dom", "feat"), None),
        ),
        out_specs=(P(("dom", "feat"), None), P(("dom", "feat"), None), P(), P()),
        check_vma=False,
    )
```

profile of v0, /device:TPU:0, one launch (start us, length us, event | category | flops | bytes accessed | tf_op | source)
XLA Modules:
  0.0 261.7 jit_solution(15932003317400076923)
XLA Ops:
  7.2 0.0 copy-start
  7.2 0.7 maximum_bitcast_fusion
  7.9 0.7 compare_bitcast_fusion
  8.6 0.1 ge.15
  8.7 1.8 gather_fusion
  10.4 0.7 copy_select_fusion
  11.2 4.2 %all-to-all-start = ((bf16[8,4,4,128]{3,2,0,1:T(4,128)(2,1)}), bf16[8,4,4,128]{3,2,0,1:T(4,128)(2,1)S(1)}, u32[]{:S(2)}, u32[]{:S(2)}) async-start(bf16[8,4,4,128]{3,2,0,1:T(4,128)(2,1)} %copy_select_fusion), calls=%async_computation | async-start | bytes 65536 | tf_op jit(solution)/shard_map/all_to_all | solution.py:25
  15.4 0.7 fusion.7
  16.0 0.7 compare_select_fusion
  16.7 0.0 copy-start.1
  16.7 0.0 copy-start.4
  16.7 8.8 %fusion.8 = (s32[96,128]{1,0:T(8,128)S(1)}, bf16[96,128,128]{2,1,0:T(8,128)(2,1)}) fusion(s32[96,128,128]{2,1,0:T(8,128)} %param.13), kind=kLoop, calls=%fused_computation.37 | loop fusion | flops 3133440 | bytes 9486336 | tf_op jit(solution)/shard_map/reduce_sum | solution.py:32
  25.5 0.0 copy-start.5
  25.6 0.0 copy-done.1
  25.6 0.0 copy-done.4
  25.6 1.8 fusion.9
  27.4 0.1 copy.43
  27.4 0.1 reshape.122
  27.5 0.0 all-to-all-done
  27.5 0.6 copy.42
  28.2 6.3 %all-to-all-start.1 = ((bf16[8,4,4,128]{3,2,1,0:T(4,128)(2,1)}), bf16[8,4,4,128]{3,2,1,0:T(4,128)(2,1)S(1)}, u32[]{:S(2)}, u32[]{:S(2)}) async-start(bf16[8,4,4,128]{3,2,1,0:T(4,128)(2,1)} %copy.42), calls=%async_computation.1 | async-start | bytes 65536 | tf_op jit(solution)/shard_map/all_to_all | solution.py:26
  34.5 0.0 copy-done.5
  34.5 0.1 copy.44
  34.6 0.6 gather_fusion.1
  35.2 0.1 reshape.130
  35.3 42.5 %all-gather.1 = bf16[32,4,128]{2,1,0:T(4,128)(2,1)S(1)} all-gather(bf16[1,4,128]{2,1,0:T(4,128)(2,1)S(1)} %bitcast.69), channel_id=2, replica_groups=mesh['dom'=8,'feat'=4] {'dom','feat'}, dimensions={0}, use_global_device_ids=true | all-gather | bytes 33792 | tf_op jit(solution)/shard_map/all_gather | solution.py:29
  77.8 0.0 all-to-all-done.1
  77.8 2.7 %gather_fusion.2 = bf16[96,128,128]{2,1,0:T(8,128)(2,1)} fusion(bf16[18,128,128]{2,1,0:T(8,128)(2,1)S(1)} %bitcast.56, s32[1024]{0:T(1024)S(1)} %pad_clamp_fusion), kind=kCustom, calls=%fused_computation.2 | custom fusion | bytes 6291840 | tf_op jit(solution)/shard_map/gather | solution.py:38
  80.5 0.0 copy-start.2
  80.5 0.0 copy-start.6
  80.5 4.0 %divide_convert_fusion.1 = bf16[16,128,128]{1,2,0:T(8,128)(2,1)S(1)} fusion(bf16[16,6,128,128]{3,2,1,0:T(8,128)(2,1)} %bitcast.57, bf16[16,6,128,128]{3,2,1,0:T(8,128)(2,1)} %bitcast.61, f32[16,128]{1,0:T(8,128)S(1)} %convert_add_fusion), kind=kOutput, calls=%fused_computation.14 | convolution fusion | flops 403177472 | bytes 6823936 | tf_op jit(solution)/shard_map/btij,btjf->bif/dot_general | solution.py:37
  84.5 0.0 copy-done
  84.5 0.0 copy-done.2
  84.5 0.0 copy-done.6
  84.5 2.2 multiply_convert_fusion
  86.7 1.0 fusion.11
  87.7 0.4 fusion.10
  88.1 1.1 convolution_bitcast_fusion.1
  89.3 0.3 copy.45
  89.6 5.5 %fusion = f32[16,128,6,128]{3,1,2,0:T(8,128)} fusion(bf16[16,6,128,128]{3,2,1,0:T(8,128)(2,1)} %bitcast.58, f32[16,128,128]{1,2,0:T(8,128)S(1)} %copy.45, f32[16,128]{1,0:T(8,128)S(1)} %convert_add_fusion), kind=kOutput, calls=%fused_computation.16 | convolution fusion | flops 403177472 | bytes 10493952 | tf_op jit(solution)/shard_map/btij,bif->btjf/dot_general | solution.py:54
  95.1 6.5 %copy.46 = f32[96,128,128]{2,1,0:T(8,128)} copy(f32[96,128,128]{1,2,0:T(8,128)} %bitcast.55) | data formatting | bytes 12582912 | tf_op jit(solution)/shard_map/reshape | solution.py:56
  101.6 0.1 broadcast_in_dim.42
  101.8 12.9 %scatter_fusion = f32[18,128,128]{2,1,0:T(8,128)S(1)} fusion(f32[18,128,128]{2,1,0:T(8,128)S(1)} %broadcast_in_dim.42, s32[96]{0:T(128)S(1)} %reshape.130, f32[96,128,128]{2,1,0:T(8,128)} %copy.46), kind=kCustom, calls=%fused_computation.3 | custom fusion | flops 1572864 | bytes 18874752 | tf_op jit(solution)/shard_map/scatter-add | solution.py:55
  114.7 0.6 copy.47
  115.3 3.3 %all-to-all-start.2 = ((bf16[8,4,4,128]{3,2,0,1:T(4,128)(2,1)}), bf16[8,4,4,128]{3,2,0,1:T(4,128)(2,1)S(1)}, u32[]{:S(2)}, u32[]{:S(2)}) async-start(bf16[8,4,4,128]{3,2,0,1:T(4,128)(2,1)} %copy.47), calls=%async_computation.2 | async-start | bytes 65536 | tf_op jit(solution)/shard_map/all_to_all | solution.py:66
  118.6 0.0 all-reduce.4.cloned.1.call-start
  118.6 0.6 slice_bitcast_fusion
  119.3 0.1 slice.28
  119.4 0.0 all-reduce.4.cloned.1.call-update
  119.4 3.1 %all-to-all-done.2 = bf16[8,4,4,128]{3,2,0,1:T(4,128)(2,1)S(1)} async-done(((bf16[8,4,4,128]{3,2,0,1:T(4,128)(2,1)}), bf16[8,4,4,128]{3,2,0,1:T(4,128)(2,1)S(1)}, u32[]{:S(2)}, u32[]{:S(2)}) %all-to-all-start.2) | async-done | bytes 32800 | tf_op jit(solution)/shard_map/all_to_all | solution.py:66
  122.5 0.6 copy.48
  123.1 3.3 %all-to-all-start.3 = ((bf16[8,4,4,128]{3,2,1,0:T(4,128)(2,1)}), bf16[8,4,4,128]{3,2,1,0:T(4,128)(2,1)S(1)}, u32[]{:S(2)}, u32[]{:S(2)}) async-start(bf16[8,4,4,128]{3,2,1,0:T(4,128)(2,1)} %copy.48), calls=%async_computation.3 | async-start | bytes 65536 | tf_op jit(solution)/shard_map/all_to_all | solution.py:67
  126.5 0.4 convolution_add_fusion.1
  126.9 6.2 %all-to-all-done.3 = bf16[8,4,4,128]{3,2,1,0:T(4,128)(2,1)S(1)} async-done(((bf16[8,4,4,128]{3,2,1,0:T(4,128)(2,1)}), bf16[8,4,4,128]{3,2,1,0:T(4,128)(2,1)S(1)}, u32[]{:S(2)}, u32[]{:S(2)}) %all-to-all-start.3) | async-done | bytes 32800 | tf_op jit(solution)/shard_map/all_to_all | solution.py:67
  133.1 1.7 scatter_custom_fusion.1
  134.8 115.5 %all-reduce.4.cloned.1.call-done = (f32[128,128]{1,0:T(8,128)}, f32[128,256]{0,1:T(8,128)}, f32[128,256]{1,0:T(8,128)}) async-done(((f32[128,128]{1,0:T(8,128)}, f32[128,256]{0,1:T(8,128)}, f32[128,256]{1,0:T(8,128)}), (f32[128,128]{1,0:T(8,128)}, f32[128,256]{0,1:T(8,128)}, f32[128,256]{1,0:T(8,128)})) %all-reduce.4.cloned.1.call-update) | async-done | bytes 327696
  250.3 1.7 copy.49
  252.0 1.2 scatter_custom_fusion.2
  253.1 0.0 copy-start.3
  253.1 1.7 copy.59
  254.9 0.0 copy-done.3
  (9 shorter events, 0.1 us)
Async XLA Ops:
  7.2 77.3 %copy-start = (bf16[128,256]{1,0:T(8,128)(2,1)S(1)}, bf16[128,256]{1,0:T(8,128)(2,1)}, u32[]{:S(2)}) copy-start(bf16[128,256]{1,0:T(8,128)(2,1)} %param.11) | copy-start | bytes 196612
  11.2 16.4 %all-to-all-start = ((bf16[8,4,4,128]{3,2,0,1:T(4,128)(2,1)}), bf16[8,4,4,128]{3,2,0,1:T(4,128)(2,1)S(1)}, u32[]{:S(2)}, u32[]{:S(2)}) async-start(bf16[8,4,4,128]{3,2,0,1:T(4,128)(2,1)} %copy_select_fusion), calls=%async_computation | async-start | bytes 65536 | tf_op jit(solution)/shard_map/all_to_all | solution.py:25
  16.7 8.8 %copy-start.1 = (bf16[2048,128]{1,0:T(8,128)(2,1)S(1)}, bf16[2048,128]{1,0:T(8,128)(2,1)}, u32[]{:S(2)}) copy-start(bf16[2048,128]{1,0:T(8,128)(2,1)} %param.8) | copy-start | bytes 1572868
  16.7 8.8 %copy-start.4 = (bf16[128,256]{1,0:T(8,128)(2,1)S(1)}, bf16[128,256]{1,0:T(8,128)(2,1)}, u32[]{:S(2)}) copy-start(bf16[128,256]{1,0:T(8,128)(2,1)} %param.10) | copy-start | bytes 196612
  25.5 9.0 %copy-start.5 = (s32[16,6]{0,1:T(8,128)S(1)}, s32[16,6]{0,1:T(8,128)}, u32[]{:S(2)}) copy-start(s32[16,6]{0,1:T(8,128)} %param.12) | copy-start | bytes 1156
  28.2 49.6 %all-to-all-start.1 = ((bf16[8,4,4,128]{3,2,1,0:T(4,128)(2,1)}), bf16[8,4,4,128]{3,2,1,0:T(4,128)(2,1)S(1)}, u32[]{:S(2)}, u32[]{:S(2)}) async-start(bf16[8,4,4,128]{3,2,1,0:T(4,128)(2,1)} %copy.42), calls=%async_computation.1 | async-start | bytes 65536 | tf_op jit(solution)/shard_map/all_to_all | solution.py:26
  80.5 4.0 %copy-start.2 = (f32[2048,256]{1,0:T(8,128)S(1)}, f32[2048,256]{1,0:T(8,128)}, u32[]{:S(2)}) copy-start(f32[2048,256]{1,0:T(8,128)} %fusion.9) | copy-start | bytes 6291460
  80.5 4.0 %copy-start.6 = (bf16[2048,256]{1,0:T(8,128)(2,1)S(1)}, bf16[2048,256]{1,0:T(8,128)(2,1)}, u32[]{:S(2)}) copy-start(bf16[2048,256]{1,0:T(8,128)(2,1)} %param.9) | copy-start | bytes 3145732
  115.3 7.2 %all-to-all-start.2 = ((bf16[8,4,4,128]{3,2,0,1:T(4,128)(2,1)}), bf16[8,4,4,128]{3,2,0,1:T(4,128)(2,1)S(1)}, u32[]{:S(2)}, u32[]{:S(2)}) async-start(bf16[8,4,4,128]{3,2,0,1:T(4,128)(2,1)} %copy.47), calls=%async_computation.2 | async-start | bytes 65536 | tf_op jit(solution)/shard_map/all_to_all | solution.py:66
  118.6 131.7 %all-reduce.4.cloned.1.call-start = ((), (), s32[]{:S(2)}) async-start(), calls=%async_computation.4 | async-start | bytes 655360
  123.1 10.0 %all-to-all-start.3 = ((bf16[8,4,4,128]{3,2,1,0:T(4,128)(2,1)}), bf16[8,4,4,128]{3,2,1,0:T(4,128)(2,1)S(1)}, u32[]{:S(2)}, u32[]{:S(2)}) async-start(bf16[8,4,4,128]{3,2,1,0:T(4,128)(2,1)} %copy.48), calls=%async_computation.3 | async-start | bytes 65536 | tf_op jit(solution)/shard_map/all_to_all | solution.py:67
  253.1 1.7 copy-start.3
Sparse Core Ops, SparseCore 0:
  125.8 124.5 all-reduce.3
where the time goes:
time: 263 us; the launch traced here: 262 us
  waiting for transfers between devices  125 us (48%)
  blocking collectives  42.5 us (16%)
  other arithmetic  28.1 us (11%)
  local copies, waits for them, and re-layouts  18.5 us (7%)
  starting transfers between devices  17.2 us (7%)
  matrix products  16.4 us (6%)
  between operations  14.3 us (5%)
    unnamed x2, waiting for transfers between devices  116 us
    all_gather x1, blocking collectives, per_device(): hub_all = lax.all_gather(hub_mine, ('dom', 'feat'), axis=0, tiled=True)  42.5 us
    scatter-add x1, other arithmetic, per_device(): jax.ops.segment_sum(pieces.reshape(blocks * tiles, block, f_width), tile_...  12.9 us
    reduce_sum x2, other arithmetic, per_device(): degree = jnp.sum(counts, axis=(1, 3)).astype(jnp.float32) + 1.0  8.8 us
    reshape x1, local copies, waits for them, and re-layouts, per_device(): pieces.reshape(blocks * tiles, block, f_width)  6.53 us
    all_to_all x1, starting transfers between devices, per_device(): lax.all_to_all(sectioned, 'dom', split_axis=0, concat_axis=0, tiled=True)  6.35 us
    all_to_all x1, waiting for transfers between devices, per_device(): lax.all_to_all(sectioned_back, 'dom', split_axis=0, concat_axis=0, tiled=...  6.2 us
    dot_general x1, matrix products, per_device(): jnp.einsum('btij,bif->btjf', weights_b, d_neigh, preferred_element_type=j...  5.5 us
  transfers between devices with their start and end apart: 5, of which 3 were waited for; matrix products, arithmetic and copies ran while one was open for 6% of the time, Pallas kernels for 0%

commit v1 on v0

v1 whole, which is shorter than its diff:
```python
import functools

import jax
import jax.numpy as jnp
from jax import lax
from jax.experimental import pallas as pl
from jax.experimental.pallas import tpu as pltpu
from jax.sharding import PartitionSpec as P

MESH = pl.DeviceIdType.MESH
F32 = jnp.float32
BF16 = jnp.bfloat16
VMEM = pl.BlockSpec(memory_space=pltpu.VMEM)


def my_place(n_feat):
    return lax.axis_index("dom") * n_feat + lax.axis_index("feat")


def place_id(q, n_feat):
    return (q // n_feat, lax.rem(q, n_feat))


def greet(n, n_feat):
    me = my_place(n_feat)
    barrier = pltpu.get_barrier_semaphore()

    def signal(d, carry):
        peer = lax.rem(me + d, n)
        pl.semaphore_signal(barrier, inc=1, device_id=place_id(peer, n_feat), device_id_type=MESH)
        return carry

    lax.fori_loop(1, n, signal, 0)
    return barrier


def send_all(n, n_feat, source_of, dest, send_sem, recv_sem):
    me = my_place(n_feat)

    def start(d, carry):
        peer = lax.rem(me + d, n)
        pltpu.make_async_remote_copy(
            src_ref=source_of(peer),
            dst_ref=dest.at[me],
            send_sem=send_sem,
            recv_sem=recv_sem,
            device_id=place_id(peer, n_feat),
            device_id_type=MESH,
        ).start()
        return carry

    lax.fori_loop(1, n, start, 0)


def wait_all(n, ref, sem):
    part = ref.at[pl.ds(0, n - 1)]
    pltpu.make_async_copy(part, part, sem).wait()


def spread_kernel(n, n_feat, ids_ref, feat_ref, recv_ref, send_ref, send_sem, recv_sem):
    barrier = greet(n, n_feat)
    me = my_place(n_feat)
    nodes = feat_ref.shape[0]
    rows = ids_ref.shape[0]
    lanes = lax.broadcasted_iota(jnp.int32, (rows, nodes), 1)
    pick = jnp.where(lanes == ids_ref[...], 1.0, 0.0).astype(BF16)
    picked = jnp.dot(pick, feat_ref[...], preferred_element_type=F32)
    send_ref[...] = picked.reshape(send_ref.shape)
    recv_ref[me] = send_ref[me]
    pl.semaphore_wait(barrier, n - 1)
    send_all(n, n_feat, lambda peer: send_ref.at[peer], recv_ref, send_sem, recv_sem)
    wait_all(n, recv_ref, recv_sem)
    wait_all(n, send_ref, send_sem)


def layer_kernel(
    n, hub_dev, src_ref, vals_ref, feat_ref, far_ref, grad_ref, ws_ref, wn_ref,
    out_ref, gf_ref, back_ref, dw_ref, source_ref, stage_ref, far_acc,
):
    step = pl.program_id(0)
    per_step, tiles, block, _ = vals_ref.shape
    near = tiles // 2
    width = ws_ref.shape[0]
    nodes = feat_ref.shape[0]
    own_blocks = nodes // block
    slots = far_ref.shape[1] - hub_dev
    halo = slots * n

    @pl.when(step == 0)
    def _():
        source_ref[:, width:] = jnp.ones((source_ref.shape[0], width), BF16)
        source_ref[:nodes, :width] = feat_ref[...]
        for p in range(n):
            stage_ref[p * slots : (p + 1) * slots] = far_ref[p, :slots]
            stage_ref[halo + p * hub_dev : halo + (p + 1) * hub_dev] = far_ref[p, slots:]
        source_ref[nodes:, :width] = stage_ref[...].astype(BF16)
        gf_ref[...] = jnp.zeros_like(gf_ref)
        far_acc[...] = jnp.zeros_like(far_acc)
        dw_ref[...] = jnp.zeros_like(dw_ref)

    weights = []
    summed = []
    for i in range(per_step):
        b = step * per_step + i
        wide = jnp.concatenate([vals_ref[i, t].astype(F32).astype(BF16) for t in range(tiles)], 1)
        picked = jnp.concatenate(
            [source_ref[pl.ds(pl.multiple_of(src_ref[b, t] * block, block), block)] for t in range(tiles)], 0
        )
        weights.append(wide)
        summed.append(jnp.dot(wide, picked, preferred_element_type=F32))
    summed = jnp.concatenate(summed, 0)
    inv = 1.0 / (summed[:, width:] + 1.0)
    neighbor = (summed[:, :width] * inv).astype(BF16)
    rows = per_step * block
    first = pl.multiple_of(step * rows, rows)
    own = feat_ref[pl.ds(first, rows)]
    both = jnp.concatenate([own, neighbor], 1)
    w_both = jnp.concatenate([ws_ref[...], wn_ref[...]], 0)
    preact = jnp.dot(both, w_both, preferred_element_type=F32)
    sigma = 0.5 * jnp.tanh(0.5 * preact) + 0.5
    out = preact * sigma
    out_ref[...] = out.astype(BF16)
    slope = sigma + out * (1.0 - sigma)
    d_pre = (grad_ref[...].astype(F32) * slope).astype(BF16)
    dw = lax.dot_general(both, d_pre, (((0,), (0,)), ((), ())), preferred_element_type=F32)
    dw_ref[0] += dw[:, :width]
    dw_ref[1] += dw[:, width:]
    d_both = lax.dot_general(d_pre, w_both, (((1,), (1,)), ((), ())), preferred_element_type=F32)
    gf_ref[pl.ds(first, rows)] += d_both[:, :width]
    d_neigh = (d_both[:, width:] * inv).astype(BF16)
    for i in range(per_step):
        b = step * per_step + i
        pieces = lax.dot_general(
            weights[i], d_neigh[i * block : (i + 1) * block], (((0,), (0,)), ((), ())),
            preferred_element_type=F32,
        )
        for t in range(tiles):
            piece = pieces[t * block : (t + 1) * block]
            if t < near:
                at = pl.ds(pl.multiple_of(src_ref[b, t] * block, block), block)
                gf_ref[at] += piece
            else:
                at = pl.ds(pl.multiple_of((src_ref[b, t] - own_blocks) * block, block), block)
                far_acc[at] += piece

    @pl.when(step == pl.num_programs(0) - 1)
    def _():
        for p in range(n):
            d_halo = far_acc[p * slots : (p + 1) * slots]
            back_ref[p, :slots] = d_halo.astype(BF16).astype(F32)
            back_ref[p, slots:] = far_acc[halo + p * hub_dev : halo + (p + 1) * hub_dev]


def collect_kernel(
    n, n_feat, ids_ref, back_ref, dw_ref, gf_ref, out_gf, out_ws, out_wn,
    recv_ref, part_ref, total_ref, full_ref, send_sem, recv_sem,
):
    barrier = greet(n, n_feat)
    me = my_place(n_feat)
    recv_ref[me] = back_ref[me]
    part_ref[me] = dw_ref[me]
    pl.semaphore_wait(barrier, n - 1)
    send_all(n, n_feat, lambda peer: dw_ref.at[peer], part_ref, send_sem.at[0], recv_sem.at[0])
    send_all(n, n_feat, lambda peer: back_ref.at[peer], recv_ref, send_sem.at[1], recv_sem.at[1])
    wait_all(n, part_ref, recv_sem.at[0])
    total_ref[...] = jnp.sum(part_ref[...], axis=0).astype(total_ref.dtype)
    full_ref[me] = total_ref[...]
    send_all(n, n_feat, lambda peer: total_ref, full_ref, send_sem.at[2], recv_sem.at[2])
    wait_all(n, recv_ref, recv_sem.at[1])
    rows = back_ref.shape[0] * back_ref.shape[1]
    width = back_ref.shape[2]
    nodes = gf_ref.shape[0]
    arrived = recv_ref[...].reshape(rows, width)
    high = arrived.astype(BF16)
    low = (arrived - high.astype(F32)).astype(BF16)
    terms = jnp.concatenate([high, low], 1)
    part = nodes // 4
    for c in range(4):
        at = lax.broadcasted_iota(jnp.int32, (part, rows), 0) + c * part
        place = jnp.where(at == ids_ref[...], 1.0, 0.0).astype(BF16)
        added = jnp.dot(place, terms, preferred_element_type=F32)
        span = pl.ds(c * part, part)
        out_gf[span] = gf_ref[span] + (added[:, :width] + added[:, width:])
    wait_all(n, full_ref, recv_sem.at[2])
    full = full_ref[...].astype(F32).reshape(2, 2, out_ws.shape[0], width)
    for h in range(2):
        out_ws[:, h * width : (h + 1) * width] = full[h, 0]
        out_wn[:, h * width : (h + 1) * width] = full[h, 1]
    wait_all(n, dw_ref, send_sem.at[0])
    wait_all(n, back_ref, send_sem.at[1])
    wait_all(n, full_ref, send_sem.at[2])


def per_device(features, grad_out, w_self, w_neigh, tile_src, tile_vals, send_rows, hub_rows):
    n_dom = lax.axis_size("dom")
    n_feat = lax.axis_size("feat")
    n = n_dom * n_feat
    nodes, width = features.shape
    hidden = w_self.shape[1]
    blocks, tiles = tile_src.shape
    block = tile_vals.shape[1]
    hub_dev = hub_rows.shape[1]
    slots = send_rows.shape[1] // n
    group = slots + hub_dev
    far = n * group
    ids = jnp.concatenate(
        [send_rows.reshape(n, slots), jnp.broadcast_to(hub_rows, (n, hub_dev))], 1
    )
    sems = pltpu.SemaphoreType.DMA

    received = pl.pallas_call(
        functools.partial(spread_kernel, n, n_feat),
        out_shape=jax.ShapeDtypeStruct((n, group, width), F32),
        in_specs=[VMEM, VMEM],
        out_specs=VMEM,
        scratch_shapes=[pltpu.VMEM((n, group, width), F32), sems, sems],
        compiler_params=pltpu.CompilerParams(
            collective_id=0, has_side_effects=True, vmem_limit_bytes=48 << 20
        ),
        name="spread_rows",
    )(ids.reshape(far, 1), features)

    per_step = 4
    steps = blocks // per_step
    rows = per_step * block
    whole = lambda s, ids: (0, 0)
    whole3 = lambda s, ids: (0, 0, 0)
    output, grad_near, back, dw = pl.pallas_call(
        functools.partial(layer_kernel, n, hub_dev),
        grid_spec=pltpu.PrefetchScalarGridSpec(
            num_scalar_prefetch=1,
            grid=(steps,),
            in_specs=[
                pl.BlockSpec((per_step, tiles, block, block), lambda s, ids: (s, 0, 0, 0)),
                pl.BlockSpec((nodes, width), whole),
                pl.BlockSpec((n, group, width), whole3),
                pl.BlockSpec((rows, hidden), lambda s, ids: (s, 0)),
                pl.BlockSpec((width, hidden), whole),
                pl.BlockSpec((width, hidden), whole),
            ],
            out_specs=[
                pl.BlockSpec((rows, hidden), lambda s, ids: (s, 0)),
                pl.BlockSpec((nodes, width), whole),
                pl.BlockSpec((n, group, width), whole3),
                pl.BlockSpec((2, 2 * width, width), whole3),
            ],
            scratch_shapes=[
                pltpu.VMEM((nodes + far, 2 * width), BF16),
                pltpu.VMEM((far, width), F32),
                pltpu.VMEM((far, width), F32),
            ],
        ),
        out_shape=[
            jax.ShapeDtypeStruct((nodes, hidden), BF16),
            jax.ShapeDtypeStruct((nodes, width), F32),
            jax.ShapeDtypeStruct((n, group, width), F32),
            jax.ShapeDtypeStruct((2, 2 * width, width), F32),
        ],
        compiler_params=pltpu.CompilerParams(
            dimension_semantics=("arbitrary",), vmem_limit_bytes=48 << 20
        ),
        name="layer_both_ways",
    )(tile_src, tile_vals.reshape(blocks, tiles, block, block), features, received, grad_out, w_self, w_neigh)

    piece = 4 * width // n
    held = BF16 if piece % 16 == 0 else F32
    grad_feat, grad_ws, grad_wn = pl.pallas_call(
        functools.partial(collect_kernel, n, n_feat),
        out_shape=[
            jax.ShapeDtypeStruct((nodes, width), F32),
            jax.ShapeDtypeStruct((width, hidden), F32),
            jax.ShapeDtypeStruct((width, hidden), F32),
        ],
        in_specs=[VMEM] * 4,
        out_specs=[VMEM] * 3,
        scratch_shapes=[
            pltpu.VMEM((n, group, width), F32),
            pltpu.VMEM((n, piece, width), F32),
            pltpu.VMEM((piece, width), held),
            pltpu.VMEM((n, piece, width), held),
            sems((3,)),
            sems((3,)),
        ],
        compiler_params=pltpu.CompilerParams(
            collective_id=1, has_side_effects=True, vmem_limit_bytes=48 << 20
        ),
        name="collect_gradients",
    )(ids.reshape(1, far), back, dw.reshape(n, piece, width), grad_near)
    return output, grad_feat, grad_ws, grad_wn


def solution(mesh):
    nodes = P(("dom", "feat"), None)
    return jax.shard_map(
        per_device,
        mesh=mesh,
        in_specs=(nodes, nodes, P(), P(), nodes, P(("dom", "feat"), None, None), nodes, nodes),
        out_specs=(nodes, nodes, P(), P()),
        check_vma=False,
    )
```

time: 263 us -> 50.2 us (0.19)
  waiting for transfers between devices: 125 us -> 0 us
  blocking collectives: 42.5 us -> 0 us
  Pallas kernels: 0 us -> 38.2 us
  other arithmetic: 28.1 us -> 1.32 us
  starting transfers between devices: 17.2 us -> 0 us
  matrix products: 16.4 us -> 0 us
  between operations: 14.3 us -> 0.69 us
  local copies, waits for them, and re-layouts: 18.5 us -> 9.54 us
    unnamed x2 -> x0, waiting for transfers between devices: 116 us -> none
    all_gather x1 -> x0, blocking collectives: 42.5 us -> none  [per_device(): hub_all = lax.all_gather(hub_mine, ('dom', 'feat'), axis=0, tiled=True)]
    pallas_call x0 -> x3, Pallas kernels: none -> 38.2 us  [the longest x1 20 us: per_device(): pl.pallas_call(functools.partial(collect_kernel, n, n_feat), out_shape=[j...]
    all_to_all x4 -> x0, starting transfers between devices: 17.1 us -> none  [the longest x1 6.35 us: per_device(): lax.all_to_all(sectioned, 'dom', split_axis=0, concat_axis=0, tiled=True)]
    dot_general x8 -> x0, matrix products: 16.4 us -> none  [the longest x1 5.5 us: per_device(): jnp.einsum('btij,bif->btjf', weights_b, d_neigh, preferred_element_type=j...]
    scatter-add x3 -> x0, other arithmetic: 15.8 us -> none  [the longest x1 12.9 us: per_device(): jax.ops.segment_sum(pieces.reshape(blocks * tiles, block, f_width), tile_...]
    all_to_all x4 -> x0, waiting for transfers between devices: 9.31 us -> none  [the longest x1 6.2 us: per_device(): lax.all_to_all(sectioned_back, 'dom', split_axis=0, concat_axis=0, tiled=...]
    reduce_sum x2 -> x0, other arithmetic: 8.8 us -> none  [per_device(): degree = jnp.sum(counts, axis=(1, 3)).astype(jnp.float32) + 1.0]
  transfers between devices with their start and end apart: 5 -> 0, of which waited for: 3 -> 0; matrix products, arithmetic and copies ran while one was open for 6% -> 0% of each run, Pallas kernels for 0% -> 0%
where the time goes in v1:
time: 50.2 us; the launch traced here: 49.8 us
  Pallas kernels  38.2 us (76%)
  local copies, waits for them, and re-layouts  9.54 us (19%)
  other arithmetic  1.32 us (3%)
  between operations  0.69 us (1%)
    pallas_call x1, Pallas kernels, per_device(): pl.pallas_call(functools.partial(collect_kernel, n, n_feat), out_shape=[j...  20 us
    pallas_call x1, Pallas kernels, per_device(): pl.pallas_call(functools.partial(spread_kernel, n, n_feat), out_shape=jax...  10.1 us
    unnamed x15, local copies, waits for them, and re-layouts  8.53 us
    pallas_call x1, Pallas kernels, per_device(): pl.pallas_call(functools.partial(layer_kernel, n, hub_dev), grid_spec=plt...  8.11 us
    unnamed x1, other arithmetic  1.32 us

profile of v1, /device:TPU:0, one launch (start us, length us, event | category | flops | bytes accessed | tf_op | source)
XLA Modules:
  0.0 49.8 jit_solution(6751910577661741289)
XLA Ops:
  0.6 0.5 %broadcast.5 = s32[]{:T(128)} broadcast(s32[]{:T(128)} %constant.4), dimensions={} | broadcast | bytes 8 | tf_op args[6]
  1.1 1.3 %reduce.3 = s32[128]{0:T(128)S(1)} reduce(s32[1,128]{1,0:T(1,128)} %param.14, s32[]{:T(128)} %broadcast.5), dimensions={0}, to_apply=%param.14.reduce_sub_computation.3 | reduce | bytes 1028 | tf_op args[6]
  2.5 0.7 %pad.1.clone = s32[8]{0:T(128)S(1)} pad(s32[4]{0:T(128)} %bitcast.5, s32[]{:T(128)} %constant.4), padding=4_0 | pad | bytes 52 | tf_op jit(solution)/shard_map/concatenate | solution.py:206
  3.2 0.8 %copy.21.src_ref = s32[16,6]{1,0:T(8,128)S(1)} copy(s32[16,6]{0,1:T(8,128)} %param.12) | data formatting | bytes 768 | tf_op args[4]
  4.0 0.1 reshape.24
  4.1 0.1 reshape.26.ids_ref
  4.2 0.1 reshape.28.ids_ref
  4.3 0.0 copy-start
  4.3 1.0 %copy-done = bf16[2048,128]{1,0:T(8,128)(2,1)S(1)} copy-done((bf16[2048,128]{1,0:T(8,128)(2,1)S(1)}, bf16[2048,128]{1,0:T(8,128)(2,1)}, u32[]{:S(2)}) %copy-start) | copy-done | bytes 524312
  5.3 10.1 %spread_rows.1.far_ref = f32[32,8,128]{2,1,0:T(8,128)S(1)} custom-call(s32[256,1]{1,0:T(8,128)S(1)} %reshape.28.ids_ref, bf16[2048,128]{1,0:T(8,128)(2,1)S(1)} %copy-done), custom_call_target="tpu_custom_call" | custom-call | tf_op jit(solution)/shard_map/spread_rows/pallas_call | solution.py:211
  15.4 0.0 copy-start.1
  15.4 1.0 %copy-done.1 = bf16[2048,128]{1,0:T(8,128)(2,1)S(1)} copy-done((bf16[2048,128]{1,0:T(8,128)(2,1)S(1)}, bf16[2048,128]{1,0:T(8,128)(2,1)}, u32[]{:S(2)}) %copy-start.1) | copy-done | bytes 524312
  16.4 0.0 copy-start.2
  16.4 1.2 %copy-done.2 = bf16[2048,256]{1,0:T(8,128)(2,1)S(1)} copy-done((bf16[2048,256]{1,0:T(8,128)(2,1)S(1)}, bf16[2048,256]{1,0:T(8,128)(2,1)}, u32[]{:S(2)}) %copy-start.2) | copy-done | bytes 1048600
  17.7 0.0 copy-start.3
  17.7 0.8 %copy-done.3 = bf16[128,256]{1,0:T(8,128)(2,1)S(1)} copy-done((bf16[128,256]{1,0:T(8,128)(2,1)S(1)}, bf16[128,256]{1,0:T(8,128)(2,1)}, u32[]{:S(2)}) %copy-start.3) | copy-done | bytes 65560
  18.5 0.0 copy-start.4
  18.5 0.8 %copy-done.4 = bf16[128,256]{1,0:T(8,128)(2,1)S(1)} copy-done((bf16[128,256]{1,0:T(8,128)(2,1)S(1)}, bf16[128,256]{1,0:T(8,128)(2,1)}, u32[]{:S(2)}) %copy-start.4) | copy-done | bytes 65560
  19.3 8.1 %layer_both_ways.1 = (bf16[2048,256]{1,0:T(8,128)(2,1)}, f32[2048,128]{1,0:T(8,128)S(1)}, f32[32,8,128]{2,1,0:T(8,128)S(1)}, f32[2,256,128]{2,1,0:T(8,128)S(1)}) custom-call(s32[16,6]{1,0:T(8,128)S(1)} %copy.21.src_ref, s32[16,6,128,128]{3,2,1,0:T(8,128)} %bitcast.4, bf16[2048,128]{1,0:T(8,128)(2,1)S(1)} %copy-done.1, f32[32,8,128]{2,1,0:T(8,128)S(1)} %spread_rows.1.far_ref, ...), custom_call_target="tpu_custom_call" | custom-call | tf_op jit(solution)/shard_map/layer_both_ways/pallas_call | solution.py:228
  27.5 20.0 %collect_gradients.1 = (f32[2048,128]{1,0:T(8,128)S(1)}, f32[128,256]{1,0:T(8,128)S(1)}, f32[128,256]{1,0:T(8,128)S(1)}) custom-call(s32[1,256]{1,0:T(1,128)S(1)} %reshape.26.ids_ref, f32[32,8,128]{2,1,0:T(8,128)S(1)} %get-tuple-element.12.back_ref, f32[32,16,128]{2,1,0:T(8,128)S(1)} %bitcast.3, f32[2048,128]{1,0:T(8,128)S(1)} %get-tuple-element.14.gf_ref), custom_call_target="tpu_custom_call" | custom-call | tf_op jit(solution)/shard_map/collect_gradients/pallas_call | solution.py:267
  47.5 1.0 %copy.25 = f32[2048,128]{1,0:T(8,128)} copy(f32[2048,128]{1,0:T(8,128)S(1)} %get-tuple-element.23) | data formatting | bytes 2097152
  48.4 0.7 %copy.26 = f32[128,256]{1,0:T(8,128)} copy(f32[128,256]{1,0:T(8,128)S(1)} %get-tuple-element.24) | data formatting | bytes 262144
  49.1 0.7 %copy.27 = f32[128,256]{1,0:T(8,128)} copy(f32[128,256]{1,0:T(8,128)S(1)} %get-tuple-element.25) | data formatting | bytes 262144
  (1 shorter events, 0.0 us)
Async XLA Ops:
  4.3 1.0 %copy-start = (bf16[2048,128]{1,0:T(8,128)(2,1)S(1)}, bf16[2048,128]{1,0:T(8,128)(2,1)}, u32[]{:S(2)}) copy-start(bf16[2048,128]{1,0:T(8,128)(2,1)} %feat_ref.3) | copy-start | bytes 1572868
  15.4 1.0 %copy-start.1 = (bf16[2048,128]{1,0:T(8,128)(2,1)S(1)}, bf16[2048,128]{1,0:T(8,128)(2,1)}, u32[]{:S(2)}) copy-start(bf16[2048,128]{1,0:T(8,128)(2,1)} %feat_ref.3) | copy-start | bytes 1572868
  16.4 1.2 %copy-start.2 = (bf16[2048,256]{1,0:T(8,128)(2,1)S(1)}, bf16[2048,256]{1,0:T(8,128)(2,1)}, u32[]{:S(2)}) copy-start(bf16[2048,256]{1,0:T(8,128)(2,1)} %grad_ref.1) | copy-start | bytes 3145732
  17.7 0.8 %copy-start.3 = (bf16[128,256]{1,0:T(8,128)(2,1)S(1)}, bf16[128,256]{1,0:T(8,128)(2,1)}, u32[]{:S(2)}) copy-start(bf16[128,256]{1,0:T(8,128)(2,1)} %ws_ref.1) | copy-start | bytes 196612
  18.5 0.8 %copy-start.4 = (bf16[128,256]{1,0:T(8,128)(2,1)S(1)}, bf16[128,256]{1,0:T(8,128)(2,1)}, u32[]{:S(2)}) copy-start(bf16[128,256]{1,0:T(8,128)(2,1)} %wn_ref.1) | copy-start | bytes 196612

commit v2 on v0

v2 whole, which is shorter than its diff:
```python
import functools

import jax
import jax.numpy as jnp
from jax import lax
from jax.experimental import pallas as pl
from jax.experimental.pallas import tpu as pltpu
from jax.sharding import PartitionSpec as P

MESH = pl.DeviceIdType.MESH
F32 = jnp.float32
BF16 = jnp.bfloat16
VMEM = pl.BlockSpec(memory_space=pltpu.VMEM)


def my_place(n_feat):
    return lax.axis_index("dom") * n_feat + lax.axis_index("feat")


def place_id(q, n_feat):
    return (q // n_feat, lax.rem(q, n_feat))


def greet(n, n_feat):
    me = my_place(n_feat)
    barrier = pltpu.get_barrier_semaphore()

    def signal(d, carry):
        peer = lax.rem(me + d, n)
        pl.semaphore_signal(barrier, inc=1, device_id=place_id(peer, n_feat), device_id_type=MESH)
        return carry

    lax.fori_loop(1, n, signal, 0)
    return barrier


def send_all(count, me, place_of, source_of, dest, send_sem, recv_sem):
    def start(d, carry):
        peer = lax.rem(me + d, count)
        pltpu.make_async_remote_copy(
            src_ref=source_of(peer),
            dst_ref=dest.at[me],
            send_sem=send_sem,
            recv_sem=recv_sem,
            device_id=place_of(peer),
            device_id_type=MESH,
        ).start()
        return carry

    lax.fori_loop(1, count, start, 0)


def wait_all(count, ref, sem):
    part = ref.at[pl.ds(0, count - 1)]
    pltpu.make_async_copy(part, part, sem).wait()


def one_hot_rows(ids_ref, first, count):
    at = lax.broadcasted_iota(jnp.int32, (count, ids_ref.shape[1]), 0) + first
    return jnp.where(at == ids_ref[...], 1.0, 0.0).astype(BF16)


OVER_ROWS = (((0,), (0,)), ((), ()))
OVER_COLS = (((1,), (1,)), ((), ()))


def spread_kernel(
    n, n_feat, per_step, send_rows, hub_rows, feat_hbm, grad_hbm, ws_hbm, wn_hbm, vals_hbm,
    source_ref, wide_ref, grad_ref, w_ref,
    feat_ref, vals_ref, stage_ref, send_ref, recv_ref, load_sem, vals_sem, send_sem, recv_sem,
):
    nodes, width = feat_ref.shape
    steps, group, block, _ = vals_ref.shape
    tiles = group // per_step
    halo, hub_dev = send_rows.shape[1], hub_rows.shape[1]
    slots = halo // n
    load_feat = pltpu.make_async_copy(feat_hbm, feat_ref, load_sem.at[0])
    load_feat.start()

    def load_vals(c):
        return pltpu.make_async_copy(vals_hbm.at[c], vals_ref.at[c], vals_sem.at[c])

    for c in range(steps):
        load_vals(c).start()
    loads = [
        pltpu.make_async_copy(grad_hbm, grad_ref, load_sem.at[1]),
        pltpu.make_async_copy(ws_hbm, w_ref.at[:width], load_sem.at[2]),
        pltpu.make_async_copy(wn_hbm, w_ref.at[width:], load_sem.at[3]),
    ]
    for load in loads:
        load.start()
    barrier = greet(n, n_feat)
    me = my_place(n_feat)
    load_feat.wait()
    feat = feat_ref[...]
    picked = lax.dot_general(one_hot_rows(send_rows, 0, nodes), feat, OVER_ROWS, preferred_element_type=F32)
    hubs = lax.dot_general(one_hot_rows(hub_rows, 0, nodes), feat, OVER_ROWS, preferred_element_type=F32)
    for p in range(n):
        send_ref[p, :slots] = picked[p * slots : (p + 1) * slots]
        send_ref[p, slots:] = hubs
    recv_ref[me] = send_ref[me]
    pl.semaphore_wait(barrier, n - 1)
    send_all(n, me, lambda q: place_id(q, n_feat), lambda q: send_ref.at[q], recv_ref, send_sem, recv_sem)
    source_ref[:nodes, :width] = feat
    source_ref[:, width:] = jnp.ones((source_ref.shape[0], width), BF16)

    def convert(c, carry):
        load_vals(c).wait()
        for i in range(per_step):
            b = c * per_step + i
            wide_ref[b] = jnp.concatenate(
                [vals_ref[c, i * tiles + t].astype(F32).astype(BF16) for t in range(tiles)], 1
            )
        return carry

    lax.fori_loop(0, steps, convert, 0)
    for load in loads:
        load.wait()
    wait_all(n, recv_ref, recv_sem)
    for p in range(n):
        stage_ref[p * slots : (p + 1) * slots] = recv_ref[p, :slots]
        stage_ref[halo + p * hub_dev : halo + (p + 1) * hub_dev] = recv_ref[p, slots:]
    source_ref[nodes:, :width] = stage_ref[...].astype(BF16)
    wait_all(n, send_ref, send_sem)


def layer_kernel(
    n, hub_dev, per_step, src_ref, source_ref, wide_ref, grad_ref, w_ref,
    out_hbm, gf_ref, back_ref, dw_ref, out_ref, far_acc, out_sem,
):
    blocks, block, reach = wide_ref.shape
    tiles = reach // block
    near = tiles // 2
    nodes, width = gf_ref.shape
    own_blocks = nodes // block
    slots = back_ref.shape[1] - hub_dev
    halo = slots * n
    gf_ref[...] = jnp.zeros_like(gf_ref)
    far_acc[...] = jnp.zeros_like(far_acc)
    dw_ref[...] = jnp.zeros_like(dw_ref)
    rows = per_step * block

    def flush(step):
        span = pl.ds(pl.multiple_of(step * rows, rows), rows)
        return pltpu.make_async_copy(out_ref.at[span], out_hbm.at[span], out_sem.at[step])

    def body(step, carry):
        summed = []
        for i in range(per_step):
            b = step * per_step + i
            picked = jnp.concatenate(
                [source_ref[pl.ds(pl.multiple_of(src_ref[b, t] * block, block), block)] for t in range(tiles)], 0
            )
            summed.append(jnp.dot(wide_ref[b], picked, preferred_element_type=F32))
        summed = jnp.concatenate(summed, 0)
        inv = 1.0 / (summed[:, width:] + 1.0)
        neighbor = (summed[:, :width] * inv).astype(BF16)
        span = pl.ds(pl.multiple_of(step * rows, rows), rows)
        both = jnp.concatenate([source_ref[span, :width], neighbor], 1)
        preact = jnp.dot(both, w_ref[...], preferred_element_type=F32)
        sigma = 0.5 * jnp.tanh(0.5 * preact) + 0.5
        out = preact * sigma
        out_ref[span] = out.astype(BF16)
        flush(step).start()
        slope = sigma + out * (1.0 - sigma)
        d_pre = (grad_ref[span].astype(F32) * slope).astype(BF16)
        d_both = lax.dot_general(d_pre, w_ref[...], OVER_COLS, preferred_element_type=F32)
        d_neigh = (d_both[:, width:] * inv).astype(BF16)
        gf_ref[span] += d_both[:, :width]
        dw = lax.dot_general(both, d_pre, OVER_ROWS, preferred_element_type=F32)
        dw_ref[0] += dw[:, :width]
        dw_ref[1] += dw[:, width:]
        for i in range(per_step):
            b = step * per_step + i
            pieces = lax.dot_general(
                wide_ref[b], d_neigh[i * block : (i + 1) * block], OVER_ROWS, preferred_element_type=F32
            )
            for t in range(tiles):
                piece = pieces[t * block : (t + 1) * block]
                if t < near:
                    at = pl.ds(pl.multiple_of(src_ref[b, t] * block, block), block)
                    gf_ref[at] += piece
                else:
                    at = pl.ds(pl.multiple_of((src_ref[b, t] - own_blocks) * block, block), block)
                    far_acc[at] += piece
        return carry

    lax.fori_loop(0, blocks // per_step, body, 0)
    for p in range(n):
        d_halo = far_acc[p * slots : (p + 1) * slots]
        back_ref[p, :slots] = d_halo.astype(BF16).astype(F32)
        back_ref[p, slots:] = far_acc[halo + p * hub_dev : halo + (p + 1) * hub_dev]
    for step in range(blocks // per_step):
        flush(step).wait()


def collect_kernel(
    n_dom, n_feat, send_rows, hub_rows, back_ref, dw_ref, gf_ref, out_gf, out_ws, out_wn,
    recv_ref, stage_ref, part_ref, mid_ref, thin_ref, small_ref, line_ref, full_ref, send_sem, recv_sem,
):
    n = n_dom * n_feat
    dom, feat = lax.axis_index("dom"), lax.axis_index("feat")
    barrier = greet(n, n_feat)
    me = my_place(n_feat)
    recv_ref[me] = back_ref[me]
    part_ref[feat] = dw_ref[feat]
    pl.semaphore_wait(barrier, n - 1)
    along = lambda q: (dom, q)
    across = lambda q: (q, feat)
    send_all(n_feat, feat, along, lambda q: dw_ref.at[q], part_ref, send_sem.at[0], recv_sem.at[0])
    send_all(n, me, lambda q: place_id(q, n_feat), lambda q: back_ref.at[q], recv_ref, send_sem.at[1], recv_sem.at[1])
    wait_all(n_feat, part_ref, recv_sem.at[0])
    mid_ref[...] = jnp.sum(part_ref[...], axis=0).reshape(mid_ref.shape)
    thin_ref[dom] = mid_ref[dom]
    send_all(n_dom, dom, across, lambda q: mid_ref.at[q], thin_ref, send_sem.at[2], recv_sem.at[2])

    wait_all(n, recv_ref, recv_sem.at[1])
    slots = back_ref.shape[1] - hub_rows.shape[1]
    width = back_ref.shape[2]
    nodes = gf_ref.shape[0]
    for p in range(n):
        stage_ref[p * slots : (p + 1) * slots] = recv_ref[p, :slots]
    terms = stage_ref[...].astype(BF16)
    hub_sum = jnp.sum(recv_ref[...], axis=0)[slots:]
    hub_high = hub_sum.astype(BF16)
    rest = hub_sum - hub_high.astype(F32)
    hub_mid = rest.astype(BF16)
    hub_low = (rest - hub_mid.astype(F32)).astype(BF16)
    hub_terms = jnp.concatenate([hub_high, hub_mid, hub_low], 1)
    part = nodes // 4

    def scatter(c):
        span = pl.ds(c * part, part)
        added = jnp.dot(one_hot_rows(send_rows, c * part, part), terms, preferred_element_type=F32)
        hubs = jnp.dot(one_hot_rows(hub_rows, c * part, part), hub_terms, preferred_element_type=F32)
        hubs = (hubs[:, :width] + hubs[:, width : 2 * width]) + hubs[:, 2 * width :]
        out_gf[span] = gf_ref[span] + (added + hubs)

    scatter(0)
    wait_all(n_dom, thin_ref, recv_sem.at[2])
    small_ref[...] = jnp.sum(thin_ref[...], axis=0).astype(small_ref.dtype)
    line_ref[dom] = small_ref[...]
    send_all(n_dom, dom, across, lambda q: small_ref, line_ref, send_sem.at[3], recv_sem.at[3])
    scatter(1)
    wait_all(n_dom, line_ref, recv_sem.at[3])
    full_ref[feat] = line_ref[...]
    send_all(n_feat, feat, along, lambda q: line_ref, full_ref, send_sem.at[4], recv_sem.at[4])
    scatter(2)
    scatter(3)
    wait_all(n_feat, full_ref, recv_sem.at[4])
    full = full_ref[...].astype(F32).reshape(2, 2, out_ws.shape[0], width)
    for h in range(2):
        out_ws[:, h * width : (h + 1) * width] = full[h, 0]
        out_wn[:, h * width : (h + 1) * width] = full[h, 1]
    wait_all(n_feat, dw_ref, send_sem.at[0])
    wait_all(n, back_ref, send_sem.at[1])
    wait_all(n_dom, mid_ref, send_sem.at[2])
    wait_all(n_dom, line_ref, send_sem.at[3])
    wait_all(n_feat, full_ref, send_sem.at[4])


def per_device(features, grad_out, w_self, w_neigh, tile_src, tile_vals, send_rows, hub_rows):
    n_dom = lax.axis_size("dom")
    n_feat = lax.axis_size("feat")
    n = n_dom * n_feat
    nodes, width = features.shape
    hidden = w_self.shape[1]
    blocks, tiles = tile_src.shape
    block = tile_vals.shape[1]
    hub_dev = hub_rows.shape[1]
    halo = send_rows.shape[1]
    group = halo // n + hub_dev
    far = n * group
    sems = pltpu.SemaphoreType.DMA
    shape = jax.ShapeDtypeStruct
    anywhere = pl.BlockSpec(memory_space=pl.ANY)
    scalars = pl.BlockSpec(memory_space=pltpu.SMEM)
    per_step = 4
    steps = blocks // per_step
    limit = 32 << 20

    source, wide, grad, w_both = pl.pallas_call(
        functools.partial(spread_kernel, n, n_feat, per_step),
        out_shape=[
            shape((nodes + far, 2 * width), BF16),
            shape((blocks, block, tiles * block), BF16),
            shape((nodes, hidden), BF16),
            shape((2 * width, hidden), BF16),
        ],
        in_specs=[VMEM, VMEM] + [anywhere] * 5,
        out_specs=[VMEM] * 4,
        scratch_shapes=[
            pltpu.VMEM((nodes, width), BF16),
            pltpu.VMEM((steps, per_step * tiles, block, block), jnp.int32),
            pltpu.VMEM((far, width), F32),
            pltpu.VMEM((n, group, width), F32),
            pltpu.VMEM((n, group, width), F32),
            sems((4,)),
            sems((steps,)),
            sems,
            sems,
        ],
        compiler_params=pltpu.CompilerParams(
            collective_id=0, has_side_effects=True, vmem_limit_bytes=limit
        ),
        name="spread_rows",
    )(
        send_rows, hub_rows, features, grad_out, w_self, w_neigh,
        tile_vals.reshape(steps, per_step * tiles, block, block),
    )

    output, grad_near, back, dw = pl.pallas_call(
        functools.partial(layer_kernel, n, hub_dev, per_step),
        out_shape=[
            shape((nodes, hidden), BF16),
            shape((nodes, width), F32),
            shape((n, group, width), F32),
            shape((2, 2 * width, width), F32),
        ],
        in_specs=[scalars] + [VMEM] * 4,
        out_specs=[anywhere] + [VMEM] * 3,
        scratch_shapes=[
            pltpu.VMEM((nodes, hidden), BF16),
            pltpu.VMEM((far, width), F32),
            sems((steps,)),
        ],
        compiler_params=pltpu.CompilerParams(vmem_limit_bytes=limit),
        name="layer_both_ways",
    )(tile_src, source, wide, grad, w_both)

    chunk = 4 * width // n_feat
    piece = chunk // n_dom
    held = BF16 if piece % 16 == 0 else F32
    grad_feat, grad_ws, grad_wn = pl.pallas_call(
        functools.partial(collect_kernel, n_dom, n_feat),
        out_shape=[shape((nodes, width), F32), shape((width, hidden), F32), shape((width, hidden), F32)],
        in_specs=[VMEM] * 5,
        out_specs=[VMEM] * 3,
        scratch_shapes=[
            pltpu.VMEM((n, group, width), F32),
            pltpu.VMEM((halo, width), F32),
            pltpu.VMEM((n_feat, chunk, width), F32),
            pltpu.VMEM((n_dom, piece, width), F32),
            pltpu.VMEM((n_dom, piece, width), F32),
            pltpu.VMEM((piece, width), held),
            pltpu.VMEM((n_dom, piece, width), held),
            pltpu.VMEM((n_feat, n_dom, piece, width), held),
            sems((5,)),
            sems((5,)),
        ],
        compiler_params=pltpu.CompilerParams(
            collective_id=1, has_side_effects=True, vmem_limit_bytes=limit
        ),
        name="collect_gradients",
    )(send_rows, hub_rows, back, dw.reshape(n_feat, chunk, width), grad_near)
    return output, grad_feat, grad_ws, grad_wn


def solution(mesh):
    nodes = P(("dom", "feat"), None)
    return jax.shard_map(
        per_device,
        mesh=mesh,
        in_specs=(nodes, nodes, P(), P(), nodes, P(("dom", "feat"), None, None), nodes, nodes),
        out_specs=(nodes, nodes, P(), P()),
        check_vma=False,
    )
```

time: 263 us -> 50.3 us (0.19)
  waiting for transfers between devices: 125 us -> 0 us
  blocking collectives: 42.5 us -> 0 us
  Pallas kernels: 0 us -> 38.2 us
  other arithmetic: 28.1 us -> 0 us
  starting transfers between devices: 17.2 us -> 0 us
  matrix products: 16.4 us -> 0 us
  between operations: 14.3 us -> 0.66 us
  local copies, waits for them, and re-layouts: 18.5 us -> 11.1 us
    unnamed x2 -> x0, waiting for transfers between devices: 116 us -> none
    all_gather x1 -> x0, blocking collectives: 42.5 us -> none  [per_device(): hub_all = lax.all_gather(hub_mine, ('dom', 'feat'), axis=0, tiled=True)]
    pallas_call x0 -> x3, Pallas kernels: none -> 38.2 us  [the longest x1 21.7 us: per_device(): pl.pallas_call(functools.partial(collect_kernel, n_dom, n_feat), out_shap...]
    all_to_all x4 -> x0, starting transfers between devices: 17.1 us -> none  [the longest x1 6.35 us: per_device(): lax.all_to_all(sectioned, 'dom', split_axis=0, concat_axis=0, tiled=True)]
    dot_general x8 -> x0, matrix products: 16.4 us -> none  [the longest x1 5.5 us: per_device(): jnp.einsum('btij,bif->btjf', weights_b, d_neigh, preferred_element_type=j...]
    scatter-add x3 -> x0, other arithmetic: 15.8 us -> none  [the longest x1 12.9 us: per_device(): jax.ops.segment_sum(pieces.reshape(blocks * tiles, block, f_width), tile_...]
    all_to_all x4 -> x0, waiting for transfers between devices: 9.31 us -> none  [the longest x1 6.2 us: per_device(): lax.all_to_all(sectioned_back, 'dom', split_axis=0, concat_axis=0, tiled=...]
    reduce_sum x2 -> x0, other arithmetic: 8.8 us -> none  [per_device(): degree = jnp.sum(counts, axis=(1, 3)).astype(jnp.float32) + 1.0]
  transfers between devices with their start and end apart: 5 -> 0, of which waited for: 3 -> 0; matrix products, arithmetic and copies ran while one was open for 6% -> 0% of each run, Pallas kernels for 0% -> 0%
where the time goes in v2:
time: 50.3 us; the launch traced here: 50 us
  Pallas kernels  38.2 us (76%)
  local copies, waits for them, and re-layouts  11.1 us (22%)
  between operations  0.66 us (1%)
    pallas_call x1, Pallas kernels, per_device(): pl.pallas_call(functools.partial(collect_kernel, n_dom, n_feat), out_shap...  21.7 us
    pallas_call x1, Pallas kernels, per_device(): pl.pallas_call(functools.partial(spread_kernel, n, n_feat, per_step), out...  11.2 us
    unnamed x18, local copies, waits for them, and re-layouts  11.1 us
    pallas_call x1, Pallas kernels, per_device(): pl.pallas_call(functools.partial(layer_kernel, n, hub_dev, per_step), out...  5.37 us

profile of v2, /device:TPU:0, one launch (start us, length us, event | category | flops | bytes accessed | tf_op | source)
XLA Modules:
  0.0 50.0 jit_solution(12872076298549591180)
XLA Ops:
  0.6 0.8 %copy.12.src_ref = s32[16,6]{1,0:T(8,128)S(1)} copy(s32[16,6]{0,1:T(8,128)} %param.12) | data formatting | bytes 768 | tf_op args[4]
  1.4 0.0 copy-start
  1.4 2.8 %copy-done = s32[96,128,128]{2,1,0:T(8,128)S(1)} copy-done((s32[96,128,128]{2,1,0:T(8,128)S(1)}, s32[96,128,128]{2,1,0:T(8,128)}, u32[]{:S(2)}) %copy-start) | copy-done | bytes 6291480
  4.2 0.0 copy-start.1
  4.2 1.2 %copy-done.1 = bf16[2048,256]{1,0:T(8,128)(2,1)S(1)} copy-done((bf16[2048,256]{1,0:T(8,128)(2,1)S(1)}, bf16[2048,256]{1,0:T(8,128)(2,1)}, u32[]{:S(2)}) %copy-start.1) | copy-done | bytes 1048600
  5.4 0.0 copy-start.2
  5.4 1.0 %copy-done.2 = bf16[2048,128]{1,0:T(8,128)(2,1)S(1)} copy-done((bf16[2048,128]{1,0:T(8,128)(2,1)S(1)}, bf16[2048,128]{1,0:T(8,128)(2,1)}, u32[]{:S(2)}) %copy-start.2) | copy-done | bytes 524312
  6.4 0.0 copy-start.3
  6.4 0.8 %copy-done.3 = bf16[128,256]{1,0:T(8,128)(2,1)S(1)} copy-done((bf16[128,256]{1,0:T(8,128)(2,1)S(1)}, bf16[128,256]{1,0:T(8,128)(2,1)}, u32[]{:S(2)}) %copy-start.3) | copy-done | bytes 65560
  7.3 0.0 copy-start.4
  7.3 0.8 %copy-done.4 = bf16[128,256]{1,0:T(8,128)(2,1)S(1)} copy-done((bf16[128,256]{1,0:T(8,128)(2,1)S(1)}, bf16[128,256]{1,0:T(8,128)(2,1)}, u32[]{:S(2)}) %copy-start.4) | copy-done | bytes 65560
  8.1 0.0 copy-start.5
  8.1 0.7 %copy-done.5 = s32[1,128]{1,0:T(1,128)S(1)} copy-done((s32[1,128]{1,0:T(1,128)S(1)}, s32[1,128]{1,0:T(1,128)}, u32[]{:S(2)}) %copy-start.5) | copy-done | bytes 536
  8.8 0.0 copy-start.6
  8.8 0.7 %copy-done.6 = s32[1,4]{1,0:T(1,128)S(1)} copy-done((s32[1,4]{1,0:T(1,128)S(1)}, s32[1,4]{1,0:T(1,128)}, u32[]{:S(2)}) %copy-start.6) | copy-done | bytes 40
  9.4 11.2 %spread_rows.1 = (bf16[2304,256]{1,0:T(8,128)(2,1)S(1)}, bf16[16,128,768]{2,1,0:T(8,128)(2,1)S(1)}, bf16[2048,256]{1,0:T(8,128)(2,1)S(1)}, bf16[256,256]{1,0:T(8,128)(2,1)S(1)}) custom-call(s32[1,128]{1,0:T(1,128)S(1)} %copy-done.5, s32[1,4]{1,0:T(1,128)S(1)} %copy-done.6, bf16[2048,128]{1,0:T(8,128)(2,1)S(1)} %copy-done.2, bf16[2048,256]{1,0:T(8,128)(2,1)S(1)} %copy-done.1, ...), custom_call_target="tpu_custom_call" | custom-call | tf_op jit(solution)/shard_map/spread_rows/pallas_call | solution.py:282
  20.6 5.4 %layer_both_ways.1 = (bf16[2048,256]{1,0:T(8,128)(2,1)}, f32[2048,128]{1,0:T(8,128)S(1)}, f32[32,8,128]{2,1,0:T(8,128)S(1)}, f32[2,256,128]{2,1,0:T(8,128)S(1)}) custom-call(s32[16,6]{1,0:T(8,128)S(1)} %copy.12.src_ref, bf16[2304,256]{1,0:T(8,128)(2,1)S(1)} %get-tuple-element.15.source_ref, bf16[16,128,768]{2,1,0:T(8,128)(2,1)S(1)} %get-tuple-element.16.wide_ref, ...), custom_call_target="tpu_custom_call" | custom-call | tf_op jit(solution)/shard_map/layer_both_ways/pallas_call | solution.py:312
  26.0 21.7 %collect_gradients.1 = (f32[2048,128]{1,0:T(8,128)S(1)}, f32[128,256]{1,0:T(8,128)S(1)}, f32[128,256]{1,0:T(8,128)S(1)}) custom-call(s32[1,128]{1,0:T(1,128)S(1)} %copy-done.5, s32[1,4]{1,0:T(1,128)S(1)} %copy-done.6, f32[32,8,128]{2,1,0:T(8,128)S(1)} %get-tuple-element.20.back_ref, f32[4,128,128]{2,1,0:T(8,128)S(1)} %bitcast.3, ...), custom_call_target="tpu_custom_call" | custom-call | tf_op jit(solution)/shard_map/collect_gradients/pallas_call | solution.py:334
  47.7 1.0 %copy.16 = f32[2048,128]{1,0:T(8,128)} copy(f32[2048,128]{1,0:T(8,128)S(1)} %get-tuple-element.31) | data formatting | bytes 2097152
  48.6 0.7 %copy.17 = f32[128,256]{1,0:T(8,128)} copy(f32[128,256]{1,0:T(8,128)S(1)} %get-tuple-element.32) | data formatting | bytes 262144
  49.3 0.7 %copy.18 = f32[128,256]{1,0:T(8,128)} copy(f32[128,256]{1,0:T(8,128)S(1)} %get-tuple-element.33) | data formatting | bytes 262144
Async XLA Ops:
  1.4 2.8 %copy-start = (s32[96,128,128]{2,1,0:T(8,128)S(1)}, s32[96,128,128]{2,1,0:T(8,128)}, u32[]{:S(2)}) copy-start(s32[96,128,128]{2,1,0:T(8,128)} %param.13) | copy-start | bytes 18874372
  4.2 1.2 %copy-start.1 = (bf16[2048,256]{1,0:T(8,128)(2,1)S(1)}, bf16[2048,256]{1,0:T(8,128)(2,1)}, u32[]{:S(2)}) copy-start(bf16[2048,256]{1,0:T(8,128)(2,1)} %grad_hbm.1) | copy-start | bytes 3145732
  5.4 1.0 %copy-start.2 = (bf16[2048,128]{1,0:T(8,128)(2,1)S(1)}, bf16[2048,128]{1,0:T(8,128)(2,1)}, u32[]{:S(2)}) copy-start(bf16[2048,128]{1,0:T(8,128)(2,1)} %feat_hbm.1) | copy-start | bytes 1572868
  6.4 0.8 %copy-start.3 = (bf16[128,256]{1,0:T(8,128)(2,1)S(1)}, bf16[128,256]{1,0:T(8,128)(2,1)}, u32[]{:S(2)}) copy-start(bf16[128,256]{1,0:T(8,128)(2,1)} %ws_hbm.1) | copy-start | bytes 196612
  7.3 0.8 %copy-start.4 = (bf16[128,256]{1,0:T(8,128)(2,1)S(1)}, bf16[128,256]{1,0:T(8,128)(2,1)}, u32[]{:S(2)}) copy-start(bf16[128,256]{1,0:T(8,128)(2,1)} %wn_hbm.1) | copy-start | bytes 196612
  8.1 0.7 %copy-start.5 = (s32[1,128]{1,0:T(1,128)S(1)}, s32[1,128]{1,0:T(1,128)}, u32[]{:S(2)}) copy-start(s32[1,128]{1,0:T(1,128)} %send_rows.3) | copy-start | bytes 1540
  8.8 0.7 %copy-start.6 = (s32[1,4]{1,0:T(1,128)S(1)}, s32[1,4]{1,0:T(1,128)}, u32[]{:S(2)}) copy-start(s32[1,4]{1,0:T(1,128)} %hub_rows.3) | copy-start | bytes 52

commit v3 on v2

--- a/solution.py
+++ b/solution.py
@@ -149,7 +149,7 @@
         for i in range(per_step):
             b = step * per_step + i
             picked = jnp.concatenate(
-                [source_ref[pl.ds(pl.multiple_of(src_ref[b, t] * block, block), block)] for t in range(tiles)], 0
+                [source_ref[pl.ds(pl.multiple_of(src_ref[t, b] * block, block), block)] for t in range(tiles)], 0
             )
             summed.append(jnp.dot(wide_ref[b], picked, preferred_element_type=F32))
         summed = jnp.concatenate(summed, 0)
@@ -178,10 +178,10 @@
             for t in range(tiles):
                 piece = pieces[t * block : (t + 1) * block]
                 if t < near:
-                    at = pl.ds(pl.multiple_of(src_ref[b, t] * block, block), block)
+                    at = pl.ds(pl.multiple_of(src_ref[t, b] * block, block), block)
                     gf_ref[at] += piece
                 else:
-                    at = pl.ds(pl.multiple_of((src_ref[b, t] - own_blocks) * block, block), block)
+                    at = pl.ds(pl.multiple_of((src_ref[t, b] - own_blocks) * block, block), block)
                     far_acc[at] += piece
         return carry
 
@@ -301,7 +301,7 @@
             sems,
         ],
         compiler_params=pltpu.CompilerParams(
-            collective_id=0, has_side_effects=True, vmem_limit_bytes=limit
+            collective_id=0, has_side_effects=True, vmem_limit_bytes=47 << 20
         ),
         name="spread_rows",
     )(
@@ -326,7 +326,7 @@
         ],
         compiler_params=pltpu.CompilerParams(vmem_limit_bytes=limit),
         name="layer_both_ways",
-    )(tile_src, source, wide, grad, w_both)
+    )(tile_src.T, source, wide, grad, w_both)
 
     chunk = 4 * width // n_feat
     piece = chunk // n_dom

time: 50.3 us -> 46.3 us (0.920)
  local copies, waits for them, and re-layouts: 11.1 us -> 7.53 us
    unnamed x18 -> x17, local copies, waits for them, and re-layouts: 11.1 us -> 7.53 us
where the time goes in v3:
time: 46.3 us; the launch traced here: 45.9 us
  Pallas kernels  37.7 us (81%)
  local copies, waits for them, and re-layouts  7.53 us (16%)
  between operations  0.68 us (1%)
    pallas_call x1, Pallas kernels, per_device(): pl.pallas_call(functools.partial(collect_kernel, n_dom, n_feat), out_shap...  21.7 us
    pallas_call x1, Pallas kernels, per_device(): pl.pallas_call(functools.partial(spread_kernel, n, n_feat, per_step), out...  10.7 us
    unnamed x17, local copies, waits for them, and re-layouts  7.53 us
    pallas_call x1, Pallas kernels, per_device(): pl.pallas_call(functools.partial(layer_kernel, n, hub_dev, per_step), out...  5.3 us

profile of v3, /device:TPU:0, one launch (start us, length us, event | category | flops | bytes accessed | tf_op | source)
XLA Modules:
  0.0 45.9 jit_solution(1935488540226957907)
XLA Ops:
  0.6 0.0 copy-start
  0.6 1.2 %copy-done = bf16[2048,256]{1,0:T(8,128)(2,1)S(1)} copy-done((bf16[2048,256]{1,0:T(8,128)(2,1)S(1)}, bf16[2048,256]{1,0:T(8,128)(2,1)}, u32[]{:S(2)}) %copy-start) | copy-done | bytes 1048600
  1.9 0.0 copy-start.1
  1.9 1.0 %copy-done.1 = bf16[2048,128]{1,0:T(8,128)(2,1)S(1)} copy-done((bf16[2048,128]{1,0:T(8,128)(2,1)S(1)}, bf16[2048,128]{1,0:T(8,128)(2,1)}, u32[]{:S(2)}) %copy-start.1) | copy-done | bytes 524312
  2.9 0.0 copy-start.2
  2.9 0.8 %copy-done.2 = bf16[128,256]{1,0:T(8,128)(2,1)S(1)} copy-done((bf16[128,256]{1,0:T(8,128)(2,1)S(1)}, bf16[128,256]{1,0:T(8,128)(2,1)}, u32[]{:S(2)}) %copy-start.2) | copy-done | bytes 65560
  3.7 0.0 copy-start.3
  3.7 0.8 %copy-done.3 = bf16[128,256]{1,0:T(8,128)(2,1)S(1)} copy-done((bf16[128,256]{1,0:T(8,128)(2,1)S(1)}, bf16[128,256]{1,0:T(8,128)(2,1)}, u32[]{:S(2)}) %copy-start.3) | copy-done | bytes 65560
  4.6 0.0 copy-start.5
  4.6 0.7 %copy-done.5 = s32[1,128]{1,0:T(1,128)S(1)} copy-done((s32[1,128]{1,0:T(1,128)S(1)}, s32[1,128]{1,0:T(1,128)}, u32[]{:S(2)}) %copy-start.5) | copy-done | bytes 536
  5.2 0.0 copy-start.6
  5.2 0.7 %copy-done.6 = s32[1,4]{1,0:T(1,128)S(1)} copy-done((s32[1,4]{1,0:T(1,128)S(1)}, s32[1,4]{1,0:T(1,128)}, u32[]{:S(2)}) %copy-start.6) | copy-done | bytes 40
  5.9 0.0 copy-start.4
  5.9 10.7 %spread_rows.1 = (bf16[2304,256]{1,0:T(8,128)(2,1)S(1)}, bf16[16,128,768]{2,1,0:T(8,128)(2,1)S(1)}, bf16[2048,256]{1,0:T(8,128)(2,1)S(1)}, bf16[256,256]{1,0:T(8,128)(2,1)S(1)}) custom-call(s32[1,128]{1,0:T(1,128)S(1)} %copy-done.5, s32[1,4]{1,0:T(1,128)S(1)} %copy-done.6, bf16[2048,128]{1,0:T(8,128)(2,1)S(1)} %copy-done.1, bf16[2048,256]{1,0:T(8,128)(2,1)S(1)} %copy-done, ...), custom_call_target="tpu_custom_call" | custom-call | tf_op jit(solution)/shard_map/spread_rows/pallas_call | solution.py:282
  16.6 0.0 copy-done.4
  16.7 5.3 %layer_both_ways.1 = (bf16[2048,256]{1,0:T(8,128)(2,1)}, f32[2048,128]{1,0:T(8,128)S(1)}, f32[32,8,128]{2,1,0:T(8,128)S(1)}, f32[2,256,128]{2,1,0:T(8,128)S(1)}) custom-call(s32[6,16]{1,0:T(8,128)S(1)} %bitcast.4, bf16[2304,256]{1,0:T(8,128)(2,1)S(1)} %get-tuple-element.15.source_ref, bf16[16,128,768]{2,1,0:T(8,128)(2,1)S(1)} %get-tuple-element.16.wide_ref, ...), custom_call_target="tpu_custom_call" | custom-call | tf_op jit(solution)/shard_map/layer_both_ways/pallas_call | solution.py:312
  22.0 21.7 %collect_gradients.1 = (f32[2048,128]{1,0:T(8,128)S(1)}, f32[128,256]{1,0:T(8,128)S(1)}, f32[128,256]{1,0:T(8,128)S(1)}) custom-call(s32[1,128]{1,0:T(1,128)S(1)} %copy-done.5, s32[1,4]{1,0:T(1,128)S(1)} %copy-done.6, f32[32,8,128]{2,1,0:T(8,128)S(1)} %get-tuple-element.20.back_ref, f32[4,128,128]{2,1,0:T(8,128)S(1)} %bitcast.3, ...), custom_call_target="tpu_custom_call" | custom-call | tf_op jit(solution)/shard_map/collect_gradients/pallas_call | solution.py:334
  43.7 1.0 %copy.15 = f32[2048,128]{1,0:T(8,128)} copy(f32[2048,128]{1,0:T(8,128)S(1)} %get-tuple-element.31) | data formatting | bytes 2097152
  44.6 0.7 %copy.16 = f32[128,256]{1,0:T(8,128)} copy(f32[128,256]{1,0:T(8,128)S(1)} %get-tuple-element.32) | data formatting | bytes 262144
  45.3 0.7 %copy.17 = f32[128,256]{1,0:T(8,128)} copy(f32[128,256]{1,0:T(8,128)S(1)} %get-tuple-element.33) | data formatting | bytes 262144
Async XLA Ops:
  0.6 1.2 %copy-start = (bf16[2048,256]{1,0:T(8,128)(2,1)S(1)}, bf16[2048,256]{1,0:T(8,128)(2,1)}, u32[]{:S(2)}) copy-start(bf16[2048,256]{1,0:T(8,128)(2,1)} %grad_hbm.1) | copy-start | bytes 3145732
  1.9 1.0 %copy-start.1 = (bf16[2048,128]{1,0:T(8,128)(2,1)S(1)}, bf16[2048,128]{1,0:T(8,128)(2,1)}, u32[]{:S(2)}) copy-start(bf16[2048,128]{1,0:T(8,128)(2,1)} %feat_hbm.1) | copy-start | bytes 1572868
  2.9 0.8 %copy-start.2 = (bf16[128,256]{1,0:T(8,128)(2,1)S(1)}, bf16[128,256]{1,0:T(8,128)(2,1)}, u32[]{:S(2)}) copy-start(bf16[128,256]{1,0:T(8,128)(2,1)} %ws_hbm.1) | copy-start | bytes 196612
  3.7 0.8 %copy-start.3 = (bf16[128,256]{1,0:T(8,128)(2,1)S(1)}, bf16[128,256]{1,0:T(8,128)(2,1)}, u32[]{:S(2)}) copy-start(bf16[128,256]{1,0:T(8,128)(2,1)} %wn_hbm.1) | copy-start | bytes 196612
  4.6 0.7 %copy-start.5 = (s32[1,128]{1,0:T(1,128)S(1)}, s32[1,128]{1,0:T(1,128)}, u32[]{:S(2)}) copy-start(s32[1,128]{1,0:T(1,128)} %send_rows.3) | copy-start | bytes 1540
  5.2 0.7 %copy-start.6 = (s32[1,4]{1,0:T(1,128)S(1)}, s32[1,4]{1,0:T(1,128)}, u32[]{:S(2)}) copy-start(s32[1,4]{1,0:T(1,128)} %hub_rows.3) | copy-start | bytes 52
  5.9 10.8 %copy-start.4 = (s32[16,6]{0,1:T(8,128)S(1)}, s32[16,6]{0,1:T(8,128)}, u32[]{:S(2)}) copy-start(s32[16,6]{0,1:T(8,128)} %param.12) | copy-start | bytes 1156

commit v4 on v3

--- a/solution.py
+++ b/solution.py
@@ -13,24 +13,20 @@
 VMEM = pl.BlockSpec(memory_space=pltpu.VMEM)
 
 
-def my_place(n_feat):
-    return lax.axis_index("dom") * n_feat + lax.axis_index("feat")
-
-
-def place_id(q, n_feat):
-    return (q // n_feat, lax.rem(q, n_feat))
-
-
-def greet(n, n_feat):
-    me = my_place(n_feat)
+def greet(n_dom, n_feat):
+    dom, feat = lax.axis_index("dom"), lax.axis_index("feat")
     barrier = pltpu.get_barrier_semaphore()
 
-    def signal(d, carry):
-        peer = lax.rem(me + d, n)
-        pl.semaphore_signal(barrier, inc=1, device_id=place_id(peer, n_feat), device_id_type=MESH)
-        return carry
-
-    lax.fori_loop(1, n, signal, 0)
+    def signal_feat(d, carry):
+        pl.semaphore_signal(barrier, inc=1, device_id=(dom, lax.rem(feat + d, n_feat)), device_id_type=MESH)
+        return carry
+
+    def signal_dom(d, carry):
+        pl.semaphore_signal(barrier, inc=1, device_id=(lax.rem(dom + d, n_dom), feat), device_id_type=MESH)
+        return carry
+
+    lax.fori_loop(1, n_feat, signal_feat, 0)
+    lax.fori_loop(1, n_dom, signal_dom, 0)
     return barrier
 
 
@@ -65,14 +61,15 @@
 
 
 def spread_kernel(
-    n, n_feat, per_step, send_rows, hub_rows, feat_hbm, grad_hbm, ws_hbm, wn_hbm, vals_hbm,
+    n_dom, n_feat, per_step, send_rows, hub_rows, feat_hbm, grad_hbm, ws_hbm, wn_hbm, vals_hbm,
     source_ref, wide_ref, grad_ref, w_ref,
-    feat_ref, vals_ref, stage_ref, send_ref, recv_ref, load_sem, vals_sem, send_sem, recv_sem,
+    feat_ref, vals_ref, stage_ref, send_ref, hop_ref, recv_ref, load_sem, vals_sem, send_sem, recv_sem,
 ):
     nodes, width = feat_ref.shape
     steps, group, block, _ = vals_ref.shape
     tiles = group // per_step
     halo, hub_dev = send_rows.shape[1], hub_rows.shape[1]
+    n = n_dom * n_feat
     slots = halo // n
     load_feat = pltpu.make_async_copy(feat_hbm, feat_ref, load_sem.at[0])
     load_feat.start()
@@ -89,18 +86,18 @@
     ]
     for load in loads:
         load.start()
-    barrier = greet(n, n_feat)
-    me = my_place(n_feat)
+    barrier = greet(n_dom, n_feat)
+    dom, at_feat = lax.axis_index("dom"), lax.axis_index("feat")
     load_feat.wait()
     feat = feat_ref[...]
     picked = lax.dot_general(one_hot_rows(send_rows, 0, nodes), feat, OVER_ROWS, preferred_element_type=F32)
     hubs = lax.dot_general(one_hot_rows(hub_rows, 0, nodes), feat, OVER_ROWS, preferred_element_type=F32)
     for p in range(n):
-        send_ref[p, :slots] = picked[p * slots : (p + 1) * slots]
-        send_ref[p, slots:] = hubs
-    recv_ref[me] = send_ref[me]
-    pl.semaphore_wait(barrier, n - 1)
-    send_all(n, me, lambda q: place_id(q, n_feat), lambda q: send_ref.at[q], recv_ref, send_sem, recv_sem)
+        send_ref[p % n_feat, p // n_feat, :slots] = picked[p * slots : (p + 1) * slots]
+        send_ref[p % n_feat, p // n_feat, slots:] = hubs
+    hop_ref[at_feat] = send_ref[at_feat]
+    pl.semaphore_wait(barrier, n_feat + n_dom - 2)
+    send_all(n_feat, at_feat, lambda q: (dom, q), lambda q: send_ref.at[q], hop_ref, send_sem.at[0], recv_sem.at[0])
     source_ref[:nodes, :width] = feat
     source_ref[:, width:] = jnp.ones((source_ref.shape[0], width), BF16)
 
@@ -113,19 +110,24 @@
             )
         return carry
 
-    lax.fori_loop(0, steps, convert, 0)
+    lax.fori_loop(0, steps // 2, convert, 0)
+    wait_all(n_feat, hop_ref, recv_sem.at[0])
+    recv_ref[dom] = hop_ref[:, dom]
+    send_all(n_dom, dom, lambda q: (q, at_feat), lambda q: hop_ref.at[:, q], recv_ref, send_sem.at[1], recv_sem.at[1])
+    lax.fori_loop(steps // 2, steps, convert, 0)
     for load in loads:
         load.wait()
-    wait_all(n, recv_ref, recv_sem)
+    wait_all(n_dom, recv_ref, recv_sem.at[1])
     for p in range(n):
-        stage_ref[p * slots : (p + 1) * slots] = recv_ref[p, :slots]
-        stage_ref[halo + p * hub_dev : halo + (p + 1) * hub_dev] = recv_ref[p, slots:]
+        stage_ref[p * slots : (p + 1) * slots] = recv_ref[p // n_feat, p % n_feat, :slots]
+        stage_ref[halo + p * hub_dev : halo + (p + 1) * hub_dev] = recv_ref[p // n_feat, p % n_feat, slots:]
     source_ref[nodes:, :width] = stage_ref[...].astype(BF16)
-    wait_all(n, send_ref, send_sem)
+    wait_all(n_feat, send_ref, send_sem.at[0])
+    wait_all(n_dom, recv_ref, send_sem.at[1])
 
 
 def layer_kernel(
-    n, hub_dev, per_step, src_ref, source_ref, wide_ref, grad_ref, w_ref,
+    n_dom, n_feat, hub_dev, per_step, src_ref, source_ref, wide_ref, grad_ref, w_ref,
     out_hbm, gf_ref, back_ref, dw_ref, out_ref, far_acc, out_sem,
 ):
     blocks, block, reach = wide_ref.shape
@@ -133,7 +135,8 @@
     near = tiles // 2
     nodes, width = gf_ref.shape
     own_blocks = nodes // block
-    slots = back_ref.shape[1] - hub_dev
+    n = n_dom * n_feat
+    slots = back_ref.shape[2] - hub_dev
     halo = slots * n
     gf_ref[...] = jnp.zeros_like(gf_ref)
     far_acc[...] = jnp.zeros_like(far_acc)
@@ -188,40 +191,42 @@
     lax.fori_loop(0, blocks // per_step, body, 0)
     for p in range(n):
         d_halo = far_acc[p * slots : (p + 1) * slots]
-        back_ref[p, :slots] = d_halo.astype(BF16).astype(F32)
-        back_ref[p, slots:] = far_acc[halo + p * hub_dev : halo + (p + 1) * hub_dev]
+        back_ref[p % n_feat, p // n_feat, :slots] = d_halo.astype(BF16).astype(F32)
+        back_ref[p % n_feat, p // n_feat, slots:] = far_acc[halo + p * hub_dev : halo + (p + 1) * hub_dev]
     for step in range(blocks // per_step):
         flush(step).wait()
 
 
 def collect_kernel(
     n_dom, n_feat, send_rows, hub_rows, back_ref, dw_ref, gf_ref, out_gf, out_ws, out_wn,
-    recv_ref, stage_ref, part_ref, mid_ref, thin_ref, small_ref, line_ref, full_ref, send_sem, recv_sem,
+    hop_ref, recv_ref, stage_ref, part_ref, mid_ref, thin_ref, small_ref, line_ref, full_ref, send_sem, recv_sem,
 ):
     n = n_dom * n_feat
     dom, feat = lax.axis_index("dom"), lax.axis_index("feat")
-    barrier = greet(n, n_feat)
-    me = my_place(n_feat)
-    recv_ref[me] = back_ref[me]
+    barrier = greet(n_dom, n_feat)
+    hop_ref[feat] = back_ref[feat]
     part_ref[feat] = dw_ref[feat]
-    pl.semaphore_wait(barrier, n - 1)
+    pl.semaphore_wait(barrier, n_feat + n_dom - 2)
     along = lambda q: (dom, q)
     across = lambda q: (q, feat)
+    send_all(n_feat, feat, along, lambda q: back_ref.at[q], hop_ref, send_sem.at[1], recv_sem.at[1])
     send_all(n_feat, feat, along, lambda q: dw_ref.at[q], part_ref, send_sem.at[0], recv_sem.at[0])
-    send_all(n, me, lambda q: place_id(q, n_feat), lambda q: back_ref.at[q], recv_ref, send_sem.at[1], recv_sem.at[1])
+    wait_all(n_feat, hop_ref, recv_sem.at[1])
+    recv_ref[dom] = hop_ref[:, dom]
+    send_all(n_dom, dom, across, lambda q: hop_ref.at[:, q], recv_ref, send_sem.at[5], recv_sem.at[5])
     wait_all(n_feat, part_ref, recv_sem.at[0])
     mid_ref[...] = jnp.sum(part_ref[...], axis=0).reshape(mid_ref.shape)
     thin_ref[dom] = mid_ref[dom]
     send_all(n_dom, dom, across, lambda q: mid_ref.at[q], thin_ref, send_sem.at[2], recv_sem.at[2])
 
-    wait_all(n, recv_ref, recv_sem.at[1])
-    slots = back_ref.shape[1] - hub_rows.shape[1]
-    width = back_ref.shape[2]
+    wait_all(n_dom, recv_ref, recv_sem.at[5])
+    slots = back_ref.shape[2] - hub_rows.shape[1]
+    width = back_ref.shape[3]
     nodes = gf_ref.shape[0]
     for p in range(n):
-        stage_ref[p * slots : (p + 1) * slots] = recv_ref[p, :slots]
+        stage_ref[p * slots : (p + 1) * slots] = recv_ref[p // n_feat, p % n_feat, :slots]
     terms = stage_ref[...].astype(BF16)
-    hub_sum = jnp.sum(recv_ref[...], axis=0)[slots:]
+    hub_sum = jnp.sum(recv_ref[...].reshape(n, -1, width), axis=0)[slots:]
     hub_high = hub_sum.astype(BF16)
     rest = hub_sum - hub_high.astype(F32)
     hub_mid = rest.astype(BF16)
@@ -253,7 +258,8 @@
         out_ws[:, h * width : (h + 1) * width] = full[h, 0]
         out_wn[:, h * width : (h + 1) * width] = full[h, 1]
     wait_all(n_feat, dw_ref, send_sem.at[0])
-    wait_all(n, back_ref, send_sem.at[1])
+    wait_all(n_feat, back_ref, send_sem.at[1])
+    wait_all(n_dom, recv_ref, send_sem.at[5])
     wait_all(n_dom, mid_ref, send_sem.at[2])
     wait_all(n_dom, line_ref, send_sem.at[3])
     wait_all(n_feat, full_ref, send_sem.at[4])
@@ -280,7 +286,7 @@
     limit = 32 << 20
 
     source, wide, grad, w_both = pl.pallas_call(
-        functools.partial(spread_kernel, n, n_feat, per_step),
+        functools.partial(spread_kernel, n_dom, n_feat, per_step),
         out_shape=[
             shape((nodes + far, 2 * width), BF16),
             shape((blocks, block, tiles * block), BF16),
@@ -293,12 +299,13 @@
             pltpu.VMEM((nodes, width), BF16),
             pltpu.VMEM((steps, per_step * tiles, block, block), jnp.int32),
             pltpu.VMEM((far, width), F32),
-            pltpu.VMEM((n, group, width), F32),
-            pltpu.VMEM((n, group, width), F32),
+            pltpu.VMEM((n_feat, n_dom, group, width), F32),
+            pltpu.VMEM((n_feat, n_dom, group, width), F32),
+            pltpu.VMEM((n_dom, n_feat, group, width), F32),
             sems((4,)),
             sems((steps,)),
-            sems,
-            sems,
+            sems((2,)),
+            sems((2,)),
         ],
         compiler_params=pltpu.CompilerParams(
             collective_id=0, has_side_effects=True, vmem_limit_bytes=47 << 20
@@ -310,11 +317,11 @@
     )
 
     output, grad_near, back, dw = pl.pallas_call(
-        functools.partial(layer_kernel, n, hub_dev, per_step),
+        functools.partial(layer_kernel, n_dom, n_feat, hub_dev, per_step),
         out_shape=[
             shape((nodes, hidden), BF16),
             shape((nodes, width), F32),
-            shape((n, group, width), F32),
+            shape((n_feat, n_dom, group, width), F32),
             shape((2, 2 * width, width), F32),
         ],
         in_specs=[scalars] + [VMEM] * 4,
@@ -337,7 +344,8 @@
         in_specs=[VMEM] * 5,
         out_specs=[VMEM] * 3,
         scratch_shapes=[
-            pltpu.VMEM((n, group, width), F32),
+            pltpu.VMEM((n_feat, n_dom, group, width), F32),
+            pltpu.VMEM((n_dom, n_feat, group, width), F32),
             pltpu.VMEM((halo, width), F32),
             pltpu.VMEM((n_feat, chunk, width), F32),
             pltpu.VMEM((n_dom, piece, width), F32),
@@ -345,8 +353,8 @@
             pltpu.VMEM((piece, width), held),
             pltpu.VMEM((n_dom, piece, width), held),
             pltpu.VMEM((n_feat, n_dom, piece, width), held),
-            sems((5,)),
-            sems((5,)),
+            sems((6,)),
+            sems((6,)),
         ],
         compiler_params=pltpu.CompilerParams(
             collective_id=1, has_side_effects=True, vmem_limit_bytes=limit

time: 46.3 us -> 48.7 us (1.052)
  Pallas kernels: 37.7 us -> 40.2 us
    pallas_call x2, Pallas kernels: 16 us -> 18.7 us  [the longest x1 13.4 us: per_device(): pl.pallas_call(functools.partial(spread_kernel, n_dom, n_feat, per_step),...]
where the time goes in v4:
time: 48.7 us; the launch traced here: 48.4 us
  Pallas kernels  40.2 us (83%)
  local copies, waits for them, and re-layouts  7.53 us (15%)
  between operations  0.68 us (1%)
    pallas_call x1, Pallas kernels, per_device(): pl.pallas_call(functools.partial(collect_kernel, n_dom, n_feat), out_shap...  21.5 us
    pallas_call x1, Pallas kernels, per_device(): pl.pallas_call(functools.partial(spread_kernel, n_dom, n_feat, per_step),...  13.4 us
    unnamed x17, local copies, waits for them, and re-layouts  7.53 us
    pallas_call x1, Pallas kernels, per_device(): pl.pallas_call(functools.partial(layer_kernel, n_dom, n_feat, hub_dev, pe...  5.3 us

profile of v4, /device:TPU:0, one launch (start us, length us, event | category | flops | bytes accessed | tf_op | source)
XLA Modules:
  0.0 48.4 jit_solution(9857919760693445951)
XLA Ops:
  0.6 0.0 copy-start
  0.6 1.2 %copy-done = bf16[2048,256]{1,0:T(8,128)(2,1)S(1)} copy-done((bf16[2048,256]{1,0:T(8,128)(2,1)S(1)}, bf16[2048,256]{1,0:T(8,128)(2,1)}, u32[]{:S(2)}) %copy-start) | copy-done | bytes 1048600
  1.9 0.0 copy-start.1
  1.9 1.0 %copy-done.1 = bf16[2048,128]{1,0:T(8,128)(2,1)S(1)} copy-done((bf16[2048,128]{1,0:T(8,128)(2,1)S(1)}, bf16[2048,128]{1,0:T(8,128)(2,1)}, u32[]{:S(2)}) %copy-start.1) | copy-done | bytes 524312
  2.9 0.0 copy-start.2
  2.9 0.8 %copy-done.2 = bf16[128,256]{1,0:T(8,128)(2,1)S(1)} copy-done((bf16[128,256]{1,0:T(8,128)(2,1)S(1)}, bf16[128,256]{1,0:T(8,128)(2,1)}, u32[]{:S(2)}) %copy-start.2) | copy-done | bytes 65560
  3.7 0.0 copy-start.3
  3.7 0.8 %copy-done.3 = bf16[128,256]{1,0:T(8,128)(2,1)S(1)} copy-done((bf16[128,256]{1,0:T(8,128)(2,1)S(1)}, bf16[128,256]{1,0:T(8,128)(2,1)}, u32[]{:S(2)}) %copy-start.3) | copy-done | bytes 65560
  4.6 0.0 copy-start.5
  4.6 0.7 %copy-done.5 = s32[1,128]{1,0:T(1,128)S(1)} copy-done((s32[1,128]{1,0:T(1,128)S(1)}, s32[1,128]{1,0:T(1,128)}, u32[]{:S(2)}) %copy-start.5) | copy-done | bytes 536
  5.2 0.0 copy-start.6
  5.2 0.7 %copy-done.6 = s32[1,4]{1,0:T(1,128)S(1)} copy-done((s32[1,4]{1,0:T(1,128)S(1)}, s32[1,4]{1,0:T(1,128)}, u32[]{:S(2)}) %copy-start.6) | copy-done | bytes 40
  5.9 0.0 copy-start.4
  5.9 13.4 %spread_rows.1 = (bf16[2304,256]{1,0:T(8,128)(2,1)S(1)}, bf16[16,128,768]{2,1,0:T(8,128)(2,1)S(1)}, bf16[2048,256]{1,0:T(8,128)(2,1)S(1)}, bf16[256,256]{1,0:T(8,128)(2,1)S(1)}) custom-call(s32[1,128]{1,0:T(1,128)S(1)} %copy-done.5, s32[1,4]{1,0:T(1,128)S(1)} %copy-done.6, bf16[2048,128]{1,0:T(8,128)(2,1)S(1)} %copy-done.1, bf16[2048,256]{1,0:T(8,128)(2,1)S(1)} %copy-done, ...), custom_call_target="tpu_custom_call" | custom-call | tf_op jit(solution)/shard_map/spread_rows/pallas_call | solution.py:288
  19.3 0.0 copy-done.4
  19.3 5.3 %layer_both_ways.1 = (bf16[2048,256]{1,0:T(8,128)(2,1)}, f32[2048,128]{1,0:T(8,128)S(1)}, f32[4,8,8,128]{3,2,1,0:T(8,128)S(1)}, f32[2,256,128]{2,1,0:T(8,128)S(1)}) custom-call(s32[6,16]{1,0:T(8,128)S(1)} %bitcast.4, bf16[2304,256]{1,0:T(8,128)(2,1)S(1)} %get-tuple-element.15.source_ref, bf16[16,128,768]{2,1,0:T(8,128)(2,1)S(1)} %get-tuple-element.16.wide_ref, ...), custom_call_target="tpu_custom_call" | custom-call | tf_op jit(solution)/shard_map/layer_both_ways/pallas_call | solution.py:319
  24.6 21.5 %collect_gradients.1 = (f32[2048,128]{1,0:T(8,128)S(1)}, f32[128,256]{1,0:T(8,128)S(1)}, f32[128,256]{1,0:T(8,128)S(1)}) custom-call(s32[1,128]{1,0:T(1,128)S(1)} %copy-done.5, s32[1,4]{1,0:T(1,128)S(1)} %copy-done.6, f32[4,8,8,128]{3,2,1,0:T(8,128)S(1)} %get-tuple-element.20.back_ref, f32[4,128,128]{2,1,0:T(8,128)S(1)} %bitcast.3, ...), custom_call_target="tpu_custom_call" | custom-call | tf_op jit(solution)/shard_map/collect_gradients/pallas_call | solution.py:341
  46.1 1.0 %copy.15 = f32[2048,128]{1,0:T(8,128)} copy(f32[2048,128]{1,0:T(8,128)S(1)} %get-tuple-element.31) | data formatting | bytes 2097152
  47.1 0.7 %copy.16 = f32[128,256]{1,0:T(8,128)} copy(f32[128,256]{1,0:T(8,128)S(1)} %get-tuple-element.32) | data formatting | bytes 262144
  47.7 0.7 %copy.17 = f32[128,256]{1,0:T(8,128)} copy(f32[128,256]{1,0:T(8,128)S(1)} %get-tuple-element.33) | data formatting | bytes 262144
Async XLA Ops:
  0.6 1.2 %copy-start = (bf16[2048,256]{1,0:T(8,128)(2,1)S(1)}, bf16[2048,256]{1,0:T(8,128)(2,1)}, u32[]{:S(2)}) copy-start(bf16[2048,256]{1,0:T(8,128)(2,1)} %grad_hbm.1) | copy-start | bytes 3145732
  1.9 1.0 %copy-start.1 = (bf16[2048,128]{1,0:T(8,128)(2,1)S(1)}, bf16[2048,128]{1,0:T(8,128)(2,1)}, u32[]{:S(2)}) copy-start(bf16[2048,128]{1,0:T(8,128)(2,1)} %feat_hbm.1) | copy-start | bytes 1572868
  2.9 0.8 %copy-start.2 = (bf16[128,256]{1,0:T(8,128)(2,1)S(1)}, bf16[128,256]{1,0:T(8,128)(2,1)}, u32[]{:S(2)}) copy-start(bf16[128,256]{1,0:T(8,128)(2,1)} %ws_hbm.1) | copy-start | bytes 196612
  3.7 0.8 %copy-start.3 = (bf16[128,256]{1,0:T(8,128)(2,1)S(1)}, bf16[128,256]{1,0:T(8,128)(2,1)}, u32[]{:S(2)}) copy-start(bf16[128,256]{1,0:T(8,128)(2,1)} %wn_hbm.1) | copy-start | bytes 196612
  4.6 0.7 %copy-start.5 = (s32[1,128]{1,0:T(1,128)S(1)}, s32[1,128]{1,0:T(1,128)}, u32[]{:S(2)}) copy-start(s32[1,128]{1,0:T(1,128)} %send_rows.3) | copy-start | bytes 1540
  5.2 0.7 %copy-start.6 = (s32[1,4]{1,0:T(1,128)S(1)}, s32[1,4]{1,0:T(1,128)}, u32[]{:S(2)}) copy-start(s32[1,4]{1,0:T(1,128)} %hub_rows.3) | copy-start | bytes 52
  5.9 13.4 %copy-start.4 = (s32[16,6]{0,1:T(8,128)S(1)}, s32[16,6]{0,1:T(8,128)}, u32[]{:S(2)}) copy-start(s32[16,6]{0,1:T(8,128)} %param.12) | copy-start | bytes 1156

commit v5 on v3

--- a/solution.py
+++ b/solution.py
@@ -208,11 +208,11 @@
     along = lambda q: (dom, q)
     across = lambda q: (q, feat)
     send_all(n_feat, feat, along, lambda q: dw_ref.at[q], part_ref, send_sem.at[0], recv_sem.at[0])
-    send_all(n, me, lambda q: place_id(q, n_feat), lambda q: back_ref.at[q], recv_ref, send_sem.at[1], recv_sem.at[1])
     wait_all(n_feat, part_ref, recv_sem.at[0])
     mid_ref[...] = jnp.sum(part_ref[...], axis=0).reshape(mid_ref.shape)
     thin_ref[dom] = mid_ref[dom]
     send_all(n_dom, dom, across, lambda q: mid_ref.at[q], thin_ref, send_sem.at[2], recv_sem.at[2])
+    send_all(n, me, lambda q: place_id(q, n_feat), lambda q: back_ref.at[q], recv_ref, send_sem.at[1], recv_sem.at[1])
 
     wait_all(n, recv_ref, recv_sem.at[1])
     slots = back_ref.shape[1] - hub_rows.shape[1]

time: 46.3 us -> 48.7 us (1.052)
  Pallas kernels: 37.7 us -> 40.2 us
    pallas_call x1, Pallas kernels: 21.7 us -> 24.2 us  [per_device(): pl.pallas_call(functools.partial(collect_kernel, n_dom, n_feat), out_shap...]
where the time goes in v5:
time: 48.7 us; the launch traced here: 48.4 us
  Pallas kernels  40.2 us (83%)
  local copies, waits for them, and re-layouts  7.53 us (15%)
  between operations  0.68 us (1%)
    pallas_call x1, Pallas kernels, per_device(): pl.pallas_call(functools.partial(collect_kernel, n_dom, n_feat), out_shap...  24.2 us
    pallas_call x1, Pallas kernels, per_device(): pl.pallas_call(functools.partial(spread_kernel, n, n_feat, per_step), out...  10.7 us
    unnamed x17, local copies, waits for them, and re-layouts  7.53 us
    pallas_call x1, Pallas kernels, per_device(): pl.pallas_call(functools.partial(layer_kernel, n, hub_dev, per_step), out...  5.3 us

profile of v5, /device:TPU:0, one launch (start us, length us, event | category | flops | bytes accessed | tf_op | source)
XLA Modules:
  0.0 48.4 jit_solution(11300432828041315869)
XLA Ops:
  0.6 0.0 copy-start
  0.6 1.2 %copy-done = bf16[2048,256]{1,0:T(8,128)(2,1)S(1)} copy-done((bf16[2048,256]{1,0:T(8,128)(2,1)S(1)}, bf16[2048,256]{1,0:T(8,128)(2,1)}, u32[]{:S(2)}) %copy-start) | copy-done | bytes 1048600
  1.9 0.0 copy-start.1
  1.9 1.0 %copy-done.1 = bf16[2048,128]{1,0:T(8,128)(2,1)S(1)} copy-done((bf16[2048,128]{1,0:T(8,128)(2,1)S(1)}, bf16[2048,128]{1,0:T(8,128)(2,1)}, u32[]{:S(2)}) %copy-start.1) | copy-done | bytes 524312
  2.9 0.0 copy-start.2
  2.9 0.8 %copy-done.2 = bf16[128,256]{1,0:T(8,128)(2,1)S(1)} copy-done((bf16[128,256]{1,0:T(8,128)(2,1)S(1)}, bf16[128,256]{1,0:T(8,128)(2,1)}, u32[]{:S(2)}) %copy-start.2) | copy-done | bytes 65560
  3.7 0.0 copy-start.3
  3.7 0.8 %copy-done.3 = bf16[128,256]{1,0:T(8,128)(2,1)S(1)} copy-done((bf16[128,256]{1,0:T(8,128)(2,1)S(1)}, bf16[128,256]{1,0:T(8,128)(2,1)}, u32[]{:S(2)}) %copy-start.3) | copy-done | bytes 65560
  4.6 0.0 copy-start.5
  4.6 0.7 %copy-done.5 = s32[1,128]{1,0:T(1,128)S(1)} copy-done((s32[1,128]{1,0:T(1,128)S(1)}, s32[1,128]{1,0:T(1,128)}, u32[]{:S(2)}) %copy-start.5) | copy-done | bytes 536
  5.2 0.0 copy-start.6
  5.2 0.7 %copy-done.6 = s32[1,4]{1,0:T(1,128)S(1)} copy-done((s32[1,4]{1,0:T(1,128)S(1)}, s32[1,4]{1,0:T(1,128)}, u32[]{:S(2)}) %copy-start.6) | copy-done | bytes 40
  5.9 0.0 copy-start.4
  5.9 10.7 %spread_rows.1 = (bf16[2304,256]{1,0:T(8,128)(2,1)S(1)}, bf16[16,128,768]{2,1,0:T(8,128)(2,1)S(1)}, bf16[2048,256]{1,0:T(8,128)(2,1)S(1)}, bf16[256,256]{1,0:T(8,128)(2,1)S(1)}) custom-call(s32[1,128]{1,0:T(1,128)S(1)} %copy-done.5, s32[1,4]{1,0:T(1,128)S(1)} %copy-done.6, bf16[2048,128]{1,0:T(8,128)(2,1)S(1)} %copy-done.1, bf16[2048,256]{1,0:T(8,128)(2,1)S(1)} %copy-done, ...), custom_call_target="tpu_custom_call" | custom-call | tf_op jit(solution)/shard_map/spread_rows/pallas_call | solution.py:282
  16.6 0.0 copy-done.4
  16.7 5.3 %layer_both_ways.1 = (bf16[2048,256]{1,0:T(8,128)(2,1)}, f32[2048,128]{1,0:T(8,128)S(1)}, f32[32,8,128]{2,1,0:T(8,128)S(1)}, f32[2,256,128]{2,1,0:T(8,128)S(1)}) custom-call(s32[6,16]{1,0:T(8,128)S(1)} %bitcast.4, bf16[2304,256]{1,0:T(8,128)(2,1)S(1)} %get-tuple-element.15.source_ref, bf16[16,128,768]{2,1,0:T(8,128)(2,1)S(1)} %get-tuple-element.16.wide_ref, ...), custom_call_target="tpu_custom_call" | custom-call | tf_op jit(solution)/shard_map/layer_both_ways/pallas_call | solution.py:312
  22.0 24.2 %collect_gradients.1 = (f32[2048,128]{1,0:T(8,128)S(1)}, f32[128,256]{1,0:T(8,128)S(1)}, f32[128,256]{1,0:T(8,128)S(1)}) custom-call(s32[1,128]{1,0:T(1,128)S(1)} %copy-done.5, s32[1,4]{1,0:T(1,128)S(1)} %copy-done.6, f32[32,8,128]{2,1,0:T(8,128)S(1)} %get-tuple-element.20.back_ref, f32[4,128,128]{2,1,0:T(8,128)S(1)} %bitcast.3, ...), custom_call_target="tpu_custom_call" | custom-call | tf_op jit(solution)/shard_map/collect_gradients/pallas_call | solution.py:334
  46.1 1.0 %copy.15 = f32[2048,128]{1,0:T(8,128)} copy(f32[2048,128]{1,0:T(8,128)S(1)} %get-tuple-element.31) | data formatting | bytes 2097152
  47.1 0.7 %copy.16 = f32[128,256]{1,0:T(8,128)} copy(f32[128,256]{1,0:T(8,128)S(1)} %get-tuple-element.32) | data formatting | bytes 262144
  47.8 0.7 %copy.17 = f32[128,256]{1,0:T(8,128)} copy(f32[128,256]{1,0:T(8,128)S(1)} %get-tuple-element.33) | data formatting | bytes 262144
Async XLA Ops:
  0.6 1.2 %copy-start = (bf16[2048,256]{1,0:T(8,128)(2,1)S(1)}, bf16[2048,256]{1,0:T(8,128)(2,1)}, u32[]{:S(2)}) copy-start(bf16[2048,256]{1,0:T(8,128)(2,1)} %grad_hbm.1) | copy-start | bytes 3145732
  1.9 1.0 %copy-start.1 = (bf16[2048,128]{1,0:T(8,128)(2,1)S(1)}, bf16[2048,128]{1,0:T(8,128)(2,1)}, u32[]{:S(2)}) copy-start(bf16[2048,128]{1,0:T(8,128)(2,1)} %feat_hbm.1) | copy-start | bytes 1572868
  2.9 0.8 %copy-start.2 = (bf16[128,256]{1,0:T(8,128)(2,1)S(1)}, bf16[128,256]{1,0:T(8,128)(2,1)}, u32[]{:S(2)}) copy-start(bf16[128,256]{1,0:T(8,128)(2,1)} %ws_hbm.1) | copy-start | bytes 196612
  3.7 0.8 %copy-start.3 = (bf16[128,256]{1,0:T(8,128)(2,1)S(1)}, bf16[128,256]{1,0:T(8,128)(2,1)}, u32[]{:S(2)}) copy-start(bf16[128,256]{1,0:T(8,128)(2,1)} %wn_hbm.1) | copy-start | bytes 196612
  4.6 0.7 %copy-start.5 = (s32[1,128]{1,0:T(1,128)S(1)}, s32[1,128]{1,0:T(1,128)}, u32[]{:S(2)}) copy-start(s32[1,128]{1,0:T(1,128)} %send_rows.3) | copy-start | bytes 1540
  5.2 0.7 %copy-start.6 = (s32[1,4]{1,0:T(1,128)S(1)}, s32[1,4]{1,0:T(1,128)}, u32[]{:S(2)}) copy-start(s32[1,4]{1,0:T(1,128)} %hub_rows.3) | copy-start | bytes 52
  5.9 10.8 %copy-start.4 = (s32[16,6]{0,1:T(8,128)S(1)}, s32[16,6]{0,1:T(8,128)}, u32[]{:S(2)}) copy-start(s32[16,6]{0,1:T(8,128)} %param.12) | copy-start | bytes 1156
